TPU v7x, 32 devices: a whole 2x2x4 slice. The times are simulated.
32 devices in a mesh: box: 32 (over z, y, x, core).
Axes of the slice: x: 2, y: 2, z: 4, core: 2. Of those that a mesh axis runs over, the one named last changes fastest.
Arguments:
- cell_state: float32 [64, 5, 32, 1024], P('box'), as said below
- swap_slots: int32 [32], P('box'), may hold values from 0 to 1, as said below
- neighbours: int32 [64, 3], P('box'), may hold values from -1 to 63, as said below
Outputs:
- new_state: float32 [64, 5, 32, 1024], P('box')
Inputs may be any that keep to these rules, and one draw needn't show every extreme that they name: `swap_slots`: each device names one of its 2 slots. `neighbours`: after the swap, device d holds the boxes of first-dimension layer d of a domain 32 layers long and two boxes wide in the second dimension; the lower first-dimension neighbour of a slot lies on device d - 1, the upper on device d + 1, the box beside in the second dimension on device d itself; -1 marks the two ends of the first dimension. `cell_state`: density, pressure and internal energy of every cell are positive.
All inputs are finite; a program needn't handle non-finite values.
Results may differ from a plain program's by a relative error of at most 0.0003.
Values sent between devices are 32-bit elements; how exact they have to be, the bound alone decides.
A program may use at most 64 MiB of HBM per device.

v0:
```python
import jax
import jax.numpy as jnp
from jax import lax
from jax.sharding import PartitionSpec as P

BZC = 32
GHOST = 4
RIEMANN_ITERS = 3


EOS_LINEAR = 0.4
EOS_QUAD = 0.1
COURANT = 0.4


def from_behind(value, axis, steps):
    count = lax.axis_size(axis)
    initial, last = (max(0, -steps), min(count, count - steps))
    return lax.ppermute(value, axis, [(source, source + steps) for source in range(initial, last)])


def from_partner(shard, axis, distance):
    return lax.ppermute(shard, axis, [(i, i ^ 1 << distance) for i in range(lax.axis_size(axis))])


def layers(values, start, stop, sweep_axis, unit):
    return lax.slice_in_dim(values, start * unit, stop * unit, axis=sweep_axis)


def roll_cells(values, offset_by):
    position = lax.broadcasted_iota(jnp.int32, values.shape, values.ndim - 1) % BZC
    inside = jnp.roll(values, -offset_by, axis=values.ndim - 1)
    if offset_by > 0:
        wrapped = jnp.roll(values, BZC - offset_by, axis=values.ndim - 1)
        return jnp.where(position + offset_by < BZC, inside, wrapped)
    wrapped = jnp.roll(values, -offset_by - BZC, axis=values.ndim - 1)
    return jnp.where(position + offset_by >= 0, inside, wrapped)


def minmod(first, second):
    return 0.5 * (jnp.sign(first) + jnp.sign(second)) * jnp.minimum(jnp.abs(first), jnp.abs(second))


def primitives(conserved):
    density = jnp.maximum(conserved[0], 0.05)
    velocity = conserved[1:4] / density
    internal = jnp.maximum(
        conserved[4] / density - 0.5 * jnp.sum(velocity * velocity, axis=0), 0.05
    )
    pressure = EOS_LINEAR * density * internal + EOS_QUAD * density * density
    return jnp.concatenate([density[None], velocity, pressure[None]], axis=0)


def fastest(conserved):
    prims = primitives(conserved)
    density = prims[0]
    sound = jnp.sqrt((EOS_QUAD * density * density + (1.0 + EOS_LINEAR) * prims[4]) / density)
    return jnp.max(jnp.abs(prims[1]) + jnp.abs(prims[2]) + jnp.abs(prims[3]) + 3.0 * sound)


def face_states(prims, sweep_axis, unit, component):
    length = prims.shape[sweep_axis] // unit
    inner = length - 8
    before = layers(prims, 0, length - 3, sweep_axis, unit)
    centre_a = layers(prims, 1, length - 2, sweep_axis, unit)
    centre_b = layers(prims, 2, length - 1, sweep_axis, unit)
    after_b = layers(prims, 3, length, sweep_axis, unit)
    faces = 7.0 / 12.0 * (centre_a + centre_b) - 1.0 / 12.0 * (before + after_b)
    faces = jnp.clip(faces, jnp.minimum(centre_a, centre_b), jnp.maximum(centre_a, centre_b))
    centre = layers(prims, 3, inner + 5, sweep_axis, unit)
    left_edge = layers(faces, 1, inner + 3, sweep_axis, unit)
    right_edge = layers(faces, 2, inner + 4, sweep_axis, unit)
    pressure = prims[4:5]
    normal = prims[component : component + 1]
    near_diff = layers(pressure, 3, length - 1, sweep_axis, unit) - layers(
        pressure, 1, length - 3, sweep_axis, unit
    )
    far_diff = layers(pressure, 4, length, sweep_axis, unit) - layers(
        pressure, 0, length - 4, sweep_axis, unit
    )
    far_sum = layers(pressure, 4, length, sweep_axis, unit) + layers(
        pressure, 0, length - 4, sweep_axis, unit
    )
    steepness = jnp.abs(near_diff) / (jnp.abs(far_diff) + 0.1 * far_sum)
    squeeze = jnp.maximum(
        layers(normal, 1, length - 3, sweep_axis, unit)
        - layers(normal, 3, length - 1, sweep_axis, unit),
        0.0,
    )
    shock = jnp.clip((steepness - 0.75) * 4.0, 0.0, 1.0) * squeeze / (squeeze + 0.2)
    widest = jnp.maximum(
        jnp.maximum(
            layers(shock, 0, inner + 2, sweep_axis, unit),
            layers(shock, 1, inner + 3, sweep_axis, unit),
        ),
        layers(shock, 2, inner + 4, sweep_axis, unit),
    )
    flatten = 1.0 - widest
    down_part = minmod(centre - left_edge, 2.0 * (right_edge - centre))
    up_part = minmod(right_edge - centre, 2.0 * (centre - left_edge))
    lower_val = centre - flatten * down_part
    upper_val = centre + flatten * up_part
    return (
        layers(upper_val, 0, inner + 1, sweep_axis, unit),
        layers(lower_val, 1, inner + 2, sweep_axis, unit),
    )


def periodic_states(prims, component):
    before = roll_cells(prims, -1)
    after_one = roll_cells(prims, 1)
    after_two = roll_cells(prims, 2)
    faces = 7.0 / 12.0 * (prims + after_one) - 1.0 / 12.0 * (before + after_two)
    faces = jnp.clip(faces, jnp.minimum(prims, after_one), jnp.maximum(prims, after_one))
    left_edge = roll_cells(faces, -1)
    pressure = prims[4:5]
    normal = prims[component : component + 1]
    near_diff = roll_cells(pressure, 1) - roll_cells(pressure, -1)
    far_diff = roll_cells(pressure, 2) - roll_cells(pressure, -2)
    far_sum = roll_cells(pressure, 2) + roll_cells(pressure, -2)
    steepness = jnp.abs(near_diff) / (jnp.abs(far_diff) + 0.1 * far_sum)
    squeeze = jnp.maximum(roll_cells(normal, -1) - roll_cells(normal, 1), 0.0)
    shock = jnp.clip((steepness - 0.75) * 4.0, 0.0, 1.0) * squeeze / (squeeze + 0.2)
    widest = jnp.maximum(jnp.maximum(roll_cells(shock, -1), shock), roll_cells(shock, 1))
    flatten = 1.0 - widest
    down_part = minmod(prims - left_edge, 2.0 * (faces - prims))
    up_part = minmod(faces - prims, 2.0 * (prims - left_edge))
    lower_val = prims - flatten * down_part
    upper_val = prims + flatten * up_part
    return (roll_cells(upper_val, -1), lower_val)


def wave_side(prims):
    density = prims[0]
    pressure = prims[4]
    internal = jnp.maximum((pressure - EOS_QUAD * density * density) / (EOS_LINEAR * density), 0.05)
    impedance = jnp.sqrt(density * (EOS_QUAD * density * density + (1.0 + EOS_LINEAR) * pressure))
    gamma_eff = 1.0 + EOS_LINEAR + EOS_QUAD * density * density / pressure
    growth = (gamma_eff + 1.0) / (2.0 * gamma_eff)
    return (density, pressure, internal, impedance, growth)


def riemann(left_state, right_state, sweep_axis):
    dens_l, pres_l, int_l, imp_l, grow_l = wave_side(left_state)
    dens_r, pres_r, int_r, imp_r, grow_r = wave_side(right_state)
    vel_l = left_state[sweep_axis]
    vel_r = right_state[sweep_axis]
    floor_p = 0.1 * jnp.minimum(pres_l, pres_r)
    p_star = (imp_r * pres_l + imp_l * pres_r + imp_l * imp_r * (vel_l - vel_r)) / (imp_l + imp_r)
    p_star = jnp.maximum(p_star, floor_p)

    def speeds(guess):
        wave_l = imp_l * jnp.sqrt(1.0 + grow_l * (guess / pres_l - 1.0))
        wave_r = imp_r * jnp.sqrt(1.0 + grow_r * (guess / pres_r - 1.0))
        return (wave_l, wave_r)

    for sweep_turn in range(RIEMANN_ITERS):
        wave_l, wave_r = speeds(p_star)
        star_l = vel_l - (p_star - pres_l) / wave_l
        star_r = vel_r + (p_star - pres_r) / wave_r
        slope_l = 2.0 * wave_l**3 / (wave_l * wave_l + imp_l * imp_l)
        slope_r = 2.0 * wave_r**3 / (wave_r * wave_r + imp_r * imp_r)
        p_star = jnp.maximum(
            p_star - slope_l * slope_r * (star_r - star_l) / (slope_l + slope_r), floor_p
        )
    wave_l, wave_r = speeds(p_star)
    star_l = vel_l - (p_star - pres_l) / wave_l
    star_r = vel_r + (p_star - pres_r) / wave_r
    u_star = (wave_l * star_l + wave_r * star_r) / (wave_l + wave_r)
    vol_l = 1.0 / dens_l - (p_star - pres_l) / (wave_l * wave_l)
    vol_r = 1.0 / dens_r - (p_star - pres_r) / (wave_r * wave_r)
    inner_l = jnp.maximum(int_l + 0.5 * (p_star + pres_l) * (1.0 / dens_l - vol_l), 0.1 * int_l)
    inner_r = jnp.maximum(int_r + 0.5 * (p_star + pres_r) * (1.0 / dens_r - vol_r), 0.1 * int_r)
    upwind = u_star >= 0.0
    dens_star = jnp.where(upwind, 1.0 / vol_l, 1.0 / vol_r)
    inner_star = jnp.where(upwind, inner_l, inner_r)
    mass = dens_star * u_star
    kinetic = u_star * u_star
    momenta = []
    for component in range(1, 4):
        if component == sweep_axis:
            momenta.append(mass * u_star + p_star)
        else:
            carried = jnp.where(upwind, left_state[component], right_state[component])
            kinetic = kinetic + carried * carried
            momenta.append(mass * carried)
    energy = u_star * (dens_star * (inner_star + 0.5 * kinetic) + p_star)
    return jnp.stack([mass] + momenta + [energy], axis=0)


def rate(conserved, low_x, high_x, low_y, high_y, ratio):
    depth = conserved.shape[1]
    side_rows = conserved.shape[2] // BZC
    extended_x = jnp.concatenate([low_x, conserved, high_x], axis=1)
    extended_y = jnp.concatenate([low_y, conserved, high_y], axis=2)
    tendency = jnp.zeros_like(conserved)
    left_state, right_state = face_states(primitives(extended_x), 1, 1, 1)
    fluxes = riemann(left_state, right_state, 1)
    tendency = tendency - ratio * (
        layers(fluxes, 1, depth + 1, 1, 1) - layers(fluxes, 0, depth, 1, 1)
    )
    left_state, right_state = face_states(primitives(extended_y), 2, BZC, 2)
    fluxes = riemann(left_state, right_state, 2)
    tendency = tendency - ratio * (
        layers(fluxes, 1, side_rows + 1, 2, BZC) - layers(fluxes, 0, side_rows, 2, BZC)
    )
    left_state, right_state = periodic_states(primitives(conserved), 3)
    fluxes = riemann(left_state, right_state, 3)
    tendency = tendency - ratio * (roll_cells(fluxes, 1) - fluxes)
    return tendency


def near_faces(box_data):
    nearby = []
    for offset_by in (1, -1):
        nearby.append(from_behind(box_data, "box", offset_by))
    return (nearby[0][:, :, -GHOST:], nearby[1][:, :, :GHOST])


def local_rate(box_data, neighbours, own_start, ratio):
    slots = box_data.shape[0]
    side_span = GHOST * BZC
    below, above = near_faces(box_data)
    lower = neighbours[:, 0]
    upper = neighbours[:, 1]
    beside = neighbours[:, 2]
    from_lower = jnp.take(below, jnp.clip(lower - own_start + slots, 0, slots - 1), axis=0)
    from_upper = jnp.take(above, jnp.clip(upper - own_start - slots, 0, slots - 1), axis=0)
    edge_low = jnp.broadcast_to(box_data[:, :, :1], from_lower.shape)
    edge_high = jnp.broadcast_to(box_data[:, :, -1:], from_upper.shape)
    low_x = jnp.where((lower < 0)[:, None, None, None], edge_low, from_lower)
    high_x = jnp.where((upper < 0)[:, None, None, None], edge_high, from_upper)
    side_index = jnp.clip(beside - own_start, 0, slots - 1)
    low_y = jnp.take(box_data[..., -side_span:], side_index, axis=0)
    high_y = jnp.take(box_data[..., :side_span], side_index, axis=0)

    def unpack_rate(bundle):
        return rate(bundle[0], bundle[1], bundle[2], bundle[3], bundle[4], ratio)

    return lax.map(unpack_rate, (box_data, low_x, high_x, low_y, high_y))


def body(cell_state, swap_slots, neighbours):
    slots = cell_state.shape[0]
    chosen_slot = swap_slots[0]
    outgoing = lax.dynamic_index_in_dim(cell_state, chosen_slot, 0, keepdims=False)
    half_bit = lax.axis_size("box").bit_length() - 2
    incoming = from_partner(outgoing, "box", half_bit)
    chosen = jnp.arange(slots, dtype=jnp.int32) == chosen_slot
    box_data = jnp.where(chosen[:, None, None, None], incoming[None], cell_state)
    local_fast = jnp.max(lax.map(fastest, box_data))
    ratio = COURANT / lax.pmax(local_fast, "box")
    own_start = lax.axis_index("box") * slots
    first = box_data + local_rate(box_data, neighbours, own_start, ratio)
    return 0.5 * (box_data + first + local_rate(first, neighbours, own_start, ratio))


def solution(mesh):
    in_specs = (P("box", None, None, None), P("box"), P("box", None))
    out_specs = P("box", None, None, None)
    return jax.shard_map(body, mesh=mesh, in_specs=in_specs, out_specs=out_specs, check_vma=False)
```

profile of v0, /device:TPU:1, one launch (start us, length us, event | category | flops | bytes accessed | tf_op | source)
XLA Modules:
  0.0 275.6 jit_solution(5814403334194903647)
XLA Ops:
  0.8 1.1 dynamic-slice_bitcast_fusion.16
  1.9 3.2 %collective-permute-start = (f32[5,32,1024]{2,1,0:T(8,128)S(1)}, f32[5,32,1024]{2,1,0:T(8,128)S(1)}, u32[]{:S(2)}, u32[]{:S(2)}) collective-permute-start(f32[5,32,1024]{2,1,0:T(8,128)S(1)} %dynamic-slice_bitcast_fusion.16), channel_id=1, source_target_pairs={{0,16},{1,17},{2,18},{3,19},{4,20},{5,21},{6,22},{7,23},{8,24},{9,... | collective-permute-start | bytes 1966088 | tf_op jit(solution)/shard_map/ppermute | solution.py:23
  5.6 28.0 %collective-permute-done = f32[5,32,1024]{2,1,0:T(8,128)S(1)} collective-permute-done((f32[5,32,1024]{2,1,0:T(8,128)S(1)}, f32[5,32,1024]{2,1,0:T(8,128)S(1)}, u32[]{:S(2)}, u32[]{:S(2)}) %collective-permute-start) | collective-permute-done | bytes 655392 | tf_op jit(solution)/shard_map/ppermute | solution.py:23
  33.6 1.3 broadcast_select_fusion
  35.0 3.1 %collective-permute-start.2 = (f32[2,5,32,1024]{3,2,1,0:T(8,128)}, f32[2,5,32,1024]{3,2,1,0:T(8,128)}, u32[]{:S(2)}, u32[]{:S(2)}) collective-permute-start(f32[2,5,32,1024]{3,2,1,0:T(8,128)} %broadcast_select_fusion), channel_id=1, source_target_pairs={{1,0},{2,1},{3,2},{4,3},{5,4},{6,5},{7,6},{8,7},{9,8},{10,9},{11,1... | collective-permute-start | bytes 3932168 | tf_op jit(solution)/shard_map/ppermute | solution.py:19
  38.1 3.1 %collective-permute-start.1 = (f32[2,5,32,1024]{3,2,1,0:T(8,128)}, f32[2,5,32,1024]{3,2,1,0:T(8,128)}, u32[]{:S(2)}, u32[]{:S(2)}) collective-permute-start(f32[2,5,32,1024]{3,2,1,0:T(8,128)} %broadcast_select_fusion), channel_id=1, source_target_pairs={{0,1},{1,2},{2,3},{3,4},{4,5},{5,6},{6,7},{7,8},{8,9},{9,10},{10,1... | collective-permute-start | bytes 3932168 | tf_op jit(solution)/shard_map/ppermute | solution.py:19
  41.2 9.0 %while.36 = (s32[]{:T(128)}, f32[2]{0:T(128)S(1)}, f32[2,5,32,1024]{3,2,1,0:T(8,128)}, s32[]{:T(128)}, s32[]{:T(128)}, /*index=5*/s32[]{}, s32[]{}) while((s32[]{:T(128)}, f32[2]{0:T(128)S(1)}, f32[2,5,32,1024]{3,2,1,0:T(8,128)}, s32[]{:T(128)}, s32[]{:T(128)}, /*index=5*/s32[]{}, s32[]{}) %tuple.359), condition=%wide.region_3.6_spmd, body=%wide.region_0.5_spmd.sunk | while | flops 983043 | bytes 2097289 | solution.py:251
  43.2 1.7 fusion.350
  47.7 1.7 fusion.350
  50.8 51.8 %pmax.7 = f32[]{:T(128)} all-reduce(f32[]{:T(128)} %reduce_max.18), channel_id=1, replica_groups=mesh['box'=32] {'box'}, use_global_device_ids=true, to_apply=%region_5.8 | all-reduce | flops 1 | bytes 8 | tf_op jit(solution)/shard_map/pmax | solution.py:252
  104.8 1.1 fusion.307
  111.7 1.2 broadcast.4793.clone
  113.0 65.6 %while.37 = (s32[]{:T(128)}, f32[2,5,32,1024]{3,2,1,0:T(8,128)}, f32[]{:T(128)}, f32[2,5,4,1024]{3,2,1,0:T(4,128)}, f32[2,5,32,1024]{3,2,1,0:T(8,128)}, /*index=...) while((s32[]{:T(128)}, f32[2,5,32,1024]{3,2,1,0:T(8,128)}, ...), condition=%wide.region_10.13_spmd, body=%wide.region_6.12_spmd.sunk | while | flops 59260928 | bytes 99735536 | solution.py:240
  132.8 1.1 multiply_add_fusion.50
  134.6 1.3 constant_dynamic-update-slice_fusion.14
  136.8 1.1 dynamic-slice_bitcast_fusion.24
  139.9 1.4 multiply_add_fusion.49
  141.4 1.7 constant_dynamic-update-slice_fusion.13
  146.2 1.4 multiply_add_fusion.48
  147.6 1.6 constant_dynamic-update-slice_fusion.12
  159.2 1.1 multiply_add_fusion.50
  161.0 1.3 constant_dynamic-update-slice_fusion.14
  163.3 1.1 dynamic-slice_bitcast_fusion.24
  166.3 1.4 multiply_add_fusion.49
  167.8 1.7 constant_dynamic-update-slice_fusion.13
  172.6 1.4 multiply_add_fusion.48
  174.0 1.6 constant_dynamic-update-slice_fusion.12
  178.6 1.7 fusion.308
  180.2 3.2 %collective-permute-start.4 = (f32[2,5,32,1024]{3,2,1,0:T(8,128)S(1)}, f32[2,5,32,1024]{3,2,1,0:T(8,128)}, u32[]{:S(2)}, u32[]{:S(2)}) collective-permute-start(f32[2,5,32,1024]{3,2,1,0:T(8,128)S(1)} %fusion.308), channel_id=1, source_target_pairs={{1,0},{2,1},{3,2},{4,3},{5,4},{6,5},{7,6},{8,7},{9,8},{10,9},{11,1... | collective-permute-start | bytes 3932168 | tf_op jit(solution)/shard_map/ppermute | solution.py:19
  183.4 3.8 %collective-permute-start.3 = (f32[2,5,32,1024]{3,2,1,0:T(8,128)S(1)}, f32[2,5,32,1024]{3,2,1,0:T(8,128)}, u32[]{:S(2)}, u32[]{:S(2)}) collective-permute-start(f32[2,5,32,1024]{3,2,1,0:T(8,128)S(1)} %fusion.308), channel_id=1, source_target_pairs={{0,1},{1,2},{2,3},{3,4},{4,5},{5,6},{6,7},{7,8},{8,9},{9,10},{10,1... | collective-permute-start | bytes 3932168 | tf_op jit(solution)/shard_map/ppermute | solution.py:19
  189.4 22.2 %collective-permute-done.4 = f32[2,5,32,1024]{3,2,1,0:T(8,128)} collective-permute-done((f32[2,5,32,1024]{3,2,1,0:T(8,128)S(1)}, f32[2,5,32,1024]{3,2,1,0:T(8,128)}, u32[]{:S(2)}, u32[]{:S(2)}) %collective-permute-start.4) | collective-permute-done | bytes 1310752 | tf_op jit(solution)/shard_map/ppermute | solution.py:19
  217.4 1.2 broadcast.4793
  218.6 53.7 %while.38 = (s32[]{:T(128)}, f32[2,5,32,1024]{3,2,1,0:T(8,128)}, f32[]{:T(128)}, f32[2,5,4,1024]{3,2,1,0:T(4,128)}, f32[2,5,32,1024]{3,2,1,0:T(8,128)S(1)}, /*in...) while((s32[]{:T(128)}, f32[2,5,32,1024]{3,2,1,0:T(8,128)}, ...), condition=%wide.region_15.18_spmd, body=%wide.region_11.17_spmd.sunk | while | flops 59260928 | bytes 91708440 | solution.py:240
  235.1 1.1 multiply_add_fusion.53
  236.8 1.3 constant_dynamic-update-slice_fusion.17
  240.8 1.4 multiply_add_fusion.52
  242.3 1.7 constant_dynamic-update-slice_fusion.16
  246.4 1.4 multiply_add_fusion.51
  247.8 1.6 constant_dynamic-update-slice_fusion.15
  250.3 1.3 fusion.388
  255.8 1.1 multiply_add_fusion.53
  257.5 1.3 constant_dynamic-update-slice_fusion.17
  261.5 1.4 multiply_add_fusion.52
  263.0 1.7 constant_dynamic-update-slice_fusion.16
  267.1 1.4 multiply_add_fusion.51
  268.5 1.6 constant_dynamic-update-slice_fusion.15
  271.0 1.3 fusion.388
  272.3 3.1 %add_multiply_fusion = f32[2,5,32,1024]{3,2,1,0:T(8,128)} fusion(f32[2,5,32,1024]{3,2,1,0:T(8,128)} %get-tuple-element.362, f32[2,5,32,1024]{3,2,1,0:T(8,128)S(1)} %get-tuple-element.1278, f32[2,5,32,1024]{3,2,1,0:T(8,128)S(1)} %copy-done, f32[5,32,1024]{2,1,0:T(8,128)} %copy-done.1, pred[2]{0:T(512)(128)(4,1)S(1)} %iota_compare_fusion), kind=kLoop, calls=%fused_computation.735 | loop fusion | flops 1310720 | bytes 5898242 | tf_op jit(solution)/shard_map/mul | solution.py:255
  (357 shorter events, 75.5 us)
Async XLA Ops:
  0.0 33.6 %copy-start = (f32[2,5,32,1024]{3,2,1,0:T(8,128)S(1)}, f32[2,5,32,1024]{3,2,1,0:T(8,128)}, u32[]{:S(2)}) copy-start(f32[2,5,32,1024]{3,2,1,0:T(8,128)} %param.13) | copy-start | bytes 3932164
  0.0 5.1 %copy-start.8 = (s32[2,3]{1,0:T(2,128)S(1)}, s32[2,3]{1,0:T(2,128)}, u32[]{:S(2)}) copy-start(s32[2,3]{1,0:T(2,128)} %param.15) | copy-start | bytes 76
  1.9 31.7 %collective-permute-start = (f32[5,32,1024]{2,1,0:T(8,128)S(1)}, f32[5,32,1024]{2,1,0:T(8,128)S(1)}, u32[]{:S(2)}, u32[]{:S(2)}) collective-permute-start(f32[5,32,1024]{2,1,0:T(8,128)S(1)} %dynamic-slice_bitcast_fusion.16), channel_id=1, source_target_pairs={{0,16},{1,17},{2,18},{3,19},{4,20},{5,21},{6,22},{7,23},{8,24},{9,... | collective-permute-start | bytes 1966088 | tf_op jit(solution)/shard_map/ppermute | solution.py:23
  33.6 145.0 %copy-start.1 = (f32[5,32,1024]{2,1,0:T(8,128)}, f32[5,32,1024]{2,1,0:T(8,128)S(1)}, u32[]{:S(2)}) copy-start(f32[5,32,1024]{2,1,0:T(8,128)S(1)} %collective-permute-done) | copy-start | bytes 1966084
  35.0 72.5 %collective-permute-start.2 = (f32[2,5,32,1024]{3,2,1,0:T(8,128)}, f32[2,5,32,1024]{3,2,1,0:T(8,128)}, u32[]{:S(2)}, u32[]{:S(2)}) collective-permute-start(f32[2,5,32,1024]{3,2,1,0:T(8,128)} %broadcast_select_fusion), channel_id=1, source_target_pairs={{1,0},{2,1},{3,2},{4,3},{5,4},{6,5},{7,6},{8,7},{9,8},{10,9},{11,1... | collective-permute-start | bytes 3932168 | tf_op jit(solution)/shard_map/ppermute | solution.py:19
  38.1 71.0 %collective-permute-start.1 = (f32[2,5,32,1024]{3,2,1,0:T(8,128)}, f32[2,5,32,1024]{3,2,1,0:T(8,128)}, u32[]{:S(2)}, u32[]{:S(2)}) collective-permute-start(f32[2,5,32,1024]{3,2,1,0:T(8,128)} %broadcast_select_fusion), channel_id=1, source_target_pairs={{0,1},{1,2},{2,3},{3,4},{4,5},{5,6},{6,7},{7,8},{8,9},{9,10},{10,1... | collective-permute-start | bytes 3932168 | tf_op jit(solution)/shard_map/ppermute | solution.py:19
  149.3 1.3 copy-start.2
  151.1 1.1 copy-start.3
  175.7 1.3 copy-start.2
  177.5 1.1 copy-start.3
  180.2 31.4 %collective-permute-start.4 = (f32[2,5,32,1024]{3,2,1,0:T(8,128)S(1)}, f32[2,5,32,1024]{3,2,1,0:T(8,128)}, u32[]{:S(2)}, u32[]{:S(2)}) collective-permute-start(f32[2,5,32,1024]{3,2,1,0:T(8,128)S(1)} %fusion.308), channel_id=1, source_target_pairs={{1,0},{2,1},{3,2},{4,3},{5,4},{6,5},{7,6},{8,7},{9,8},{10,9},{11,1... | collective-permute-start | bytes 3932168 | tf_op jit(solution)/shard_map/ppermute | solution.py:19
  183.4 30.8 %collective-permute-start.3 = (f32[2,5,32,1024]{3,2,1,0:T(8,128)S(1)}, f32[2,5,32,1024]{3,2,1,0:T(8,128)}, u32[]{:S(2)}, u32[]{:S(2)}) collective-permute-start(f32[2,5,32,1024]{3,2,1,0:T(8,128)S(1)} %fusion.308), channel_id=1, source_target_pairs={{0,1},{1,2},{2,3},{3,4},{4,5},{5,6},{6,7},{7,8},{8,9},{9,10},{10,1... | collective-permute-start | bytes 3932168 | tf_op jit(solution)/shard_map/ppermute | solution.py:19
  238.8 0.9 copy-start.4
  238.8 1.0 copy-start.5
  244.0 0.9 copy-start.6
  244.1 1.0 copy-start.7
  259.5 0.9 copy-start.4
  259.5 1.0 copy-start.5
  264.8 0.9 copy-start.6
  264.8 1.0 copy-start.7
where the time goes:
time: 279 us; the launch traced here: 276 us
  other arithmetic  87.7 us (31%)
  blocking collectives  51.8 us (19%)
  waiting for transfers between devices  51.1 us (18%)
  local copies, waits for them, and re-layouts  40 us (14%)
  loops' own time  26.6 us (10%)
  starting transfers between devices  16.4 us (6%)
    pmax x1, blocking collectives, body(): ratio = COURANT / lax.pmax(local_fast, 'box')  51.8 us
    ppermute x1, waiting for transfers between devices, from_partner(): lax.ppermute(shard, axis, [(i, i ^ 1 << distance) for i in range(lax.axis...  28 us
    another operation x2, loops' own time, local_rate(): return lax.map(unpack_rate, (box_data, low_x, high_x, low_y, high_y))  26.6 us
    ppermute x4, waiting for transfers between devices, from_behind(): lax.ppermute(value, axis, [(source, source + steps) for source in range(i...  23.1 us
    while x48, other arithmetic  20.1 us
    ppermute x4, starting transfers between devices, from_behind(): lax.ppermute(value, axis, [(source, source + steps) for source in range(i...  13.2 us
    add x8, other arithmetic, face_states(): upper_val = centre + flatten * up_part  11.3 us
    another operation x12, other arithmetic, riemann(): return jnp.stack([mass] + momenta + [energy], axis=0)  7.35 us
  transfers between devices with their start and end apart: 5, of which 3 were waited for; matrix products, arithmetic and copies ran while one was open for 7% of the time, Pallas kernels for 0%

commit v1 on v0

v1 whole, which is shorter than its diff:
```python
import functools

import jax
import jax.numpy as jnp
from jax import lax
from jax.experimental import pallas as pl
from jax.experimental.pallas import tpu as pltpu
from jax.sharding import PartitionSpec as P

BZC = 32
GHOST = 4
RIEMANN_ITERS = 3
COURANT = 0.4


def rcp(x):
    return pl.reciprocal(x, approx=True)


def primitives(u):
    density = jnp.maximum(u[0], 0.05)
    inv = 1.0 / density
    v1, v2, v3 = u[1] * inv, u[2] * inv, u[3] * inv
    internal = jnp.maximum(u[4] * inv - 0.5 * (v1 * v1 + v2 * v2 + v3 * v3), 0.05)
    pressure = density * (0.4 * internal + 0.1 * density)
    return density, v1, v2, v3, pressure


def signal_speed(q):
    sound = jnp.sqrt(0.1 * q[0] + 1.4 * q[4] / q[0])
    return jnp.abs(q[1]) + jnp.abs(q[2]) + jnp.abs(q[3]) + 3.0 * sound


def clip_to(x, span):
    return jnp.minimum(jnp.maximum(x, jnp.minimum(span, 0.0)), jnp.maximum(span, 0.0))


def face_offset(d_low, d, d_high):
    return clip_to(0.5 * d + (d_low - d_high) * (1.0 / 12.0), d)


def shock(near, far, far_sum, squeeze):
    steep = jnp.abs(near) * rcp(jnp.abs(far) + 0.1 * far_sum)
    squeeze = jnp.maximum(squeeze, 0.0)
    return jnp.clip(4.0 * steep - 3.0, 0.0, 1.0) * squeeze * rcp(squeeze + 0.2)


def edges(q, a, b, flat):
    lower = q - flat * clip_to(b + b, a)
    upper = q + flat * clip_to(a + a, b)
    return lower, upper


def wave_side(r, p):
    t = 0.1 * r * r
    c2 = r * (t + 1.4 * p)
    slope = 0.5 * r * (2.4 + t * rcp(p))
    return c2, slope, c2 - slope * p


def riemann(left, right, axis):
    r_l, u_l, p_l = left[0], left[axis], left[4]
    r_r, u_r, p_r = right[0], right[axis], right[4]
    c2_l, b_l, a_l = wave_side(r_l, p_l)
    c2_r, b_r, a_r = wave_side(r_r, p_r)
    c_l = c2_l * lax.rsqrt(c2_l)
    c_r = c2_r * lax.rsqrt(c2_r)
    floor_p = 0.1 * jnp.minimum(p_l, p_r)
    guess = (c_r * p_l + c_l * p_r + c_l * c_r * (u_l - u_r)) * rcp(c_l + c_r)
    guess = jnp.maximum(guess, floor_p)
    for _ in range(RIEMANN_ITERS):
        i_l = lax.rsqrt(a_l + b_l * guess)
        i_r = lax.rsqrt(a_r + b_r * guess)
        star_l = u_l - (guess - p_l) * i_l
        star_r = u_r + (guess - p_r) * i_r
        y_l = i_l + i_l * (c2_l * (i_l * i_l))
        y_r = i_r + i_r * (c2_r * (i_r * i_r))
        guess = jnp.maximum(guess - 2.0 * (star_r - star_l) * rcp(y_l + y_r), floor_p)
    w2_l = a_l + b_l * guess
    w2_r = a_r + b_r * guess
    w_l = w2_l * lax.rsqrt(w2_l)
    w_r = w2_r * lax.rsqrt(w2_r)
    u = (w_l * u_l + w_r * u_r + (p_l - p_r)) * rcp(w_l + w_r)
    upwind = u >= 0.0
    pick = lambda x, y: jnp.where(upwind, x, y)
    r, p, w2 = pick(r_l, r_r), pick(p_l, p_r), pick(w2_l, w2_r)
    inv_r = rcp(r)
    internal = jnp.maximum(2.5 * p * inv_r - 0.25 * r, 0.05)
    drop = (guess - p) * rcp(w2)
    inner = jnp.maximum(internal + 0.5 * (guess + p) * drop, 0.1 * internal)
    mass = u * rcp(inv_r - drop)
    kinetic = u * u
    momenta = []
    for component in (1, 2, 3):
        if component == axis:
            momenta.append(mass * u + guess)
        else:
            carried = pick(left[component], right[component])
            kinetic = kinetic + carried * carried
            momenta.append(mass * carried)
    return [mass] + momenta + [mass * (inner + 0.5 * kinetic) + u * guess]


def z_shift(x, n):
    z = lax.broadcasted_iota(jnp.int32, x.shape, x.ndim - 1) % BZC
    inside = pltpu.roll(x, (-n) % 128, x.ndim - 1)
    around = pltpu.roll(x, ((BZC if n > 0 else -BZC) - n) % 128, x.ndim - 1)
    keep = z < BZC - n if n > 0 else z >= -n
    return jnp.where(keep, inside, around)


def y_shift(x, n):
    lane = lax.broadcasted_iota(jnp.int32, x.shape, 2)
    row = lax.broadcasted_iota(jnp.int32, x.shape, 1)
    turned = pltpu.roll(x, (-n * BZC) % 128, 2)
    moved = pltpu.roll(turned, 7 if n > 0 else 1, 1)
    other = jnp.concatenate([moved[1:], moved[:1]], axis=0)
    carry = jnp.where(row == (7 if n > 0 else 0), other, moved)
    keep = lane < 128 - n * BZC if n > 0 else lane >= -n * BZC
    return jnp.where(keep, turned, carry)


def plane_sweep(q, shift, axis):
    d = [shift(x, 1) - x for x in q]
    d_low = [shift(x, -1) for x in d]
    d_high = [shift(x, 1) for x in d]
    b = [face_offset(l, m, h) for l, m, h in zip(d_low, d, d_high)]
    a = [shift(m - x, -1) for m, x in zip(d, b)]
    p_high = q[4] + (d[4] + d_high[4])
    p_low = shift(q[4], -2)
    chi = shock(d[4] + d_low[4], p_high - p_low, p_high + p_low, -(d[axis] + d_low[axis]))
    flat = 1.0 - jnp.maximum(jnp.maximum(shift(chi, -1), chi), shift(chi, 1))
    pairs = [edges(*x, flat) for x in zip(q, a, b)]
    flux = riemann([shift(x[1], -1) for x in pairs], [x[0] for x in pairs], axis)
    return [shift(x, 1) - x for x in flux]


def rate_kernel(last, ratio_ref, u_ref, base_ref, out_ref, q_ref, t_ref, a_ref, chi_ref, up_ref, flux_ref):
    depth = out_ref.shape[2]
    ratio = ratio_ref[0]

    @pl.loop(0, depth + 2 * GHOST)
    def _(e):
        q = primitives([u_ref[:, f, e] for f in range(5)])
        for f in range(5):
            q_ref[f, e] = q[f]

    @pl.loop(0, depth)
    def _(x):
        q = [q_ref[f, x + GHOST] for f in range(5)]
        dz = plane_sweep(q, z_shift, 3)
        dy = plane_sweep(q, y_shift, 2)
        for f in range(5):
            t_ref[f, x] = dz[f] + dy[f]

    def chi_at(e):
        low, high = q_ref[4, e - 2], q_ref[4, e + 2]
        return shock(
            q_ref[4, e + 1] - q_ref[4, e - 1], high - low, high + low, q_ref[1, e - 1] - q_ref[1, e + 1]
        )

    def cell(e):
        chi_next = chi_at(e + 1)
        flat = 1.0 - jnp.maximum(jnp.maximum(chi_ref[0], chi_ref[1]), chi_next)
        chi_ref[0] = chi_ref[1]
        chi_ref[1] = chi_next
        lower, upper = [], []
        for f in range(5):
            q = [q_ref[f, e + k] for k in (-1, 0, 1, 2)]
            d = q[2] - q[1]
            b = face_offset(q[1] - q[0], d, q[3] - q[2])
            low, high = edges(q[1], a_ref[f], b, flat)
            a_ref[f] = d - b
            lower.append(low)
            upper.append(high)
        return lower, upper

    for f in range(5):
        q = [q_ref[f, k] for k in (1, 2, 3, 4)]
        d = q[2] - q[1]
        a_ref[f] = d - face_offset(q[1] - q[0], d, q[3] - q[2])
    chi_ref[0] = chi_at(2)
    chi_ref[1] = chi_at(3)
    _, upper = cell(3)
    for f in range(5):
        up_ref[f] = upper[f]

    def face(e):
        lower, upper = cell(e)
        flux = riemann([up_ref[f] for f in range(5)], lower, 1)
        for f in range(5):
            up_ref[f] = upper[f]
        return flux

    flux = face(GHOST)
    for f in range(5):
        flux_ref[f] = flux[f]

    @pl.loop(0, depth)
    def _(x):
        flux = face(x + GHOST + 1)
        for f in range(5):
            u = u_ref[:, f, x + GHOST]
            new = u - ratio * (flux[f] - flux_ref[f] + t_ref[f, x])
            if last:
                new = 0.5 * (base_ref[:, f, x] + new)
            out_ref[:, f, x] = new
            flux_ref[f] = flux[f]


def rate_step(last, ratio, extended, base):
    slots, fields, depth = extended.shape[0], extended.shape[1], extended.shape[2] - 2 * GHOST
    tile = (slots, 8, 128)
    vmem = pl.BlockSpec(memory_space=pltpu.VMEM)
    return pl.pallas_call(
        functools.partial(rate_kernel, last),
        out_shape=jax.ShapeDtypeStruct((slots, fields, depth, 8, 128), jnp.float32),
        in_specs=[pl.BlockSpec(memory_space=pltpu.SMEM), vmem, vmem],
        out_specs=vmem,
        scratch_shapes=[
            pltpu.VMEM((fields, depth + 2 * GHOST) + tile, jnp.float32),
            pltpu.VMEM((fields, depth) + tile, jnp.float32),
            pltpu.VMEM((fields,) + tile, jnp.float32),
            pltpu.VMEM((2,) + tile, jnp.float32),
            pltpu.VMEM((fields,) + tile, jnp.float32),
            pltpu.VMEM((fields,) + tile, jnp.float32),
        ],
        compiler_params=pltpu.CompilerParams(vmem_limit_bytes=40 * 2**20),
    )(ratio, extended, base)


def extend(box_data, neighbours, own_start):
    slots = box_data.shape[0]
    count = lax.axis_size("box")
    below = lax.ppermute(box_data[:, :, -GHOST:], "box", [(i, i + 1) for i in range(count - 1)])
    above = lax.ppermute(box_data[:, :, :GHOST], "box", [(i + 1, i) for i in range(count - 1)])
    lower, upper = neighbours[:, 0], neighbours[:, 1]
    from_lower = jnp.take(below, jnp.clip(lower - own_start + slots, 0, slots - 1), axis=0)
    from_upper = jnp.take(above, jnp.clip(upper - own_start - slots, 0, slots - 1), axis=0)
    end = lambda x: (x < 0)[:, None, None, None, None]
    low = jnp.where(end(lower), box_data[:, :, :1], from_lower)
    high = jnp.where(end(upper), box_data[:, :, -1:], from_upper)
    return jnp.concatenate([low, box_data, high], axis=2)


def body(cell_state, swap_slots, neighbours):
    slots, fields, depth, _ = cell_state.shape
    cells = cell_state.reshape(slots, fields, depth, 8, 128)
    chosen_slot = swap_slots[0]
    count = lax.axis_size("box")
    outgoing = lax.dynamic_index_in_dim(cells, chosen_slot, 0, keepdims=False)
    incoming = lax.ppermute(outgoing, "box", [(i, i ^ (count // 2)) for i in range(count)])
    fast = jnp.max(signal_speed(primitives([cells[:, f] for f in range(fields)])))
    ratio = (COURANT / lax.pmax(fast, "box")).reshape(1)
    chosen = jnp.arange(slots, dtype=jnp.int32) == chosen_slot
    box_data = jnp.where(chosen[:, None, None, None, None], incoming[None], cells)
    own_start = lax.axis_index("box") * slots
    first = rate_step(False, ratio, extend(box_data, neighbours, own_start), box_data)
    new = rate_step(True, ratio, extend(first, neighbours, own_start), box_data)
    return new.reshape(cell_state.shape)


def solution(mesh):
    in_specs = (P("box", None, None, None), P("box"), P("box", None))
    out_specs = P("box", None, None, None)
    return jax.shard_map(body, mesh=mesh, in_specs=in_specs, out_specs=out_specs, check_vma=False)
```

time: 279 us -> 136 us (0.49)
  the two profiles are of different devices: /device:TPU:1 before, /device:TPU:3 now
where the time goes in v1:
time: 136 us
  Pallas kernels  54.2 us (40%)
  blocking collectives  49.5 us (36%)
  starting transfers between devices  14 us (10%)
  waiting for transfers between devices  9.38 us (7%)
  local copies, waits for them, and re-layouts  5.19 us (4%)
  other arithmetic  2.07 us (2%)
  between operations  1.59 us (1%)
    pallas_call x2, Pallas kernels, rate_step(): pl.pallas_call(functools.partial(rate_kernel, last), out_shape=jax.ShapeD...  54.2 us
    pmax x1, blocking collectives, body(): ratio = (COURANT / lax.pmax(fast, 'box')).reshape(1)  49.5 us
    ppermute x2, waiting for transfers between devices, extend(): lax.ppermute(box_data[:, :, :GHOST], 'box', [(i + 1, i) for i in range(co...  9.07 us
    ppermute x2, starting transfers between devices, extend(): lax.ppermute(box_data[:, :, -GHOST:], 'box', [(i, i + 1) for i in range(c...  7.32 us
    ppermute x2, starting transfers between devices, extend(): lax.ppermute(box_data[:, :, :GHOST], 'box', [(i + 1, i) for i in range(co...  4.33 us
  transfers between devices with their start and end apart: 5, of which 3 were waited for; matrix products, arithmetic and copies ran while one was open for 2% of the time, Pallas kernels for 0%

profile of v1, /device:TPU:3, one launch (start us, length us, event | category | flops | bytes accessed | tf_op | source)
XLA Modules:
  0.0 135.9 jit_solution(13209768722320488960)
XLA Ops:
  0.7 1.6 %copy.12 = f32[40,8,8,128]{3,2,1,0:T(8,128)S(1)} copy(f32[40,8,8,128]{3,1,2,0:T(8,128)} %bitcast.84) | data formatting | bytes 2621440
  2.2 0.0 copy-start
  2.3 0.1 dynamic-slice_bitcast_fusion
  2.3 2.4 %collective-permute-start = (f32[5,32,8,128]{3,2,1,0:T(8,128)S(1)}, f32[5,32,8,128]{3,2,1,0:T(8,128)S(1)}, u32[]{:S(2)}, u32[]{:S(2)}) collective-permute-start(f32[5,32,8,128]{3,2,1,0:T(8,128)S(1)} %dynamic-slice_bitcast_fusion), channel_id=1, source_target_pairs={{0,16},{1,17},{2,18},{3,19},{4,20},{5,21},{6,22},{7,23},{8,24},{9,... | collective-permute-start | bytes 1966088 | tf_op jit(solution)/shard_map/ppermute | solution.py:252
  4.7 0.9 add_reduce_fusion
  5.6 0.0 copy-done
  5.6 0.2 clamp_reduce_fusion.1
  5.8 49.5 %pmax.7 = f32[]{:T(128)} all-reduce(f32[]{:T(128)} %add_reduce_fusion), channel_id=1, replica_groups=mesh['box'=32] {'box'}, use_global_device_ids=true, to_apply=%region_1.2 | all-reduce | flops 1 | bytes 8 | tf_op jit(solution)/shard_map/pmax | solution.py:254
  56.0 0.2 compare_reduce_fusion.1
  56.2 0.0 collective-permute-done
  56.3 0.2 broadcast_select_fusion.base_ref
  56.5 5.4 %collective-permute-start.1 = (f32[2,5,4,8,128]{4,3,2,1,0:T(8,128)S(1)}, f32[2,5,4,8,128]{4,3,2,1,0:T(8,128)S(1)}, u32[]{:S(2)}, u32[]{:S(2)}) collective-permute-start(f32[2,5,4,8,128]{4,3,2,1,0:T(8,128)S(1)} %get-tuple-element.16), channel_id=1, source_target_pairs={{0,1},{1,2},{2,3},{3,4},{4,5},{5,6},{6,7},{7,8},{8,9},{9,10},{10,1... | collective-permute-start | bytes 491528 | tf_op jit(solution)/shard_map/ppermute | solution.py:235
  61.9 1.9 %collective-permute-start.2 = (f32[2,5,4,8,128]{4,3,2,1,0:T(8,128)S(1)}, f32[2,5,4,8,128]{4,3,2,1,0:T(8,128)S(1)}, u32[]{:S(2)}, u32[]{:S(2)}) collective-permute-start(f32[2,5,4,8,128]{4,3,2,1,0:T(8,128)S(1)} %get-tuple-element.17), channel_id=1, source_target_pairs={{1,0},{2,1},{3,2},{4,3},{5,4},{6,5},{7,6},{8,7},{9,8},{10,9},{11,1... | collective-permute-start | bytes 491528 | tf_op jit(solution)/shard_map/ppermute | solution.py:236
  63.8 0.3 collective-permute-done.1
  64.1 0.6 gather_fusion
  64.7 0.1 select_select_fusion.3
  64.8 4.6 %collective-permute-done.2 = f32[2,5,4,8,128]{4,3,2,1,0:T(8,128)S(1)} collective-permute-done((f32[2,5,4,8,128]{4,3,2,1,0:T(8,128)S(1)}, f32[2,5,4,8,128]{4,3,2,1,0:T(8,128)S(1)}, u32[]{:S(2)}, u32[]{:S(2)}) %collective-permute-start.2) | collective-permute-done | bytes 163872 | tf_op jit(solution)/shard_map/ppermute | solution.py:236
  69.4 0.6 gather_fusion.1
  70.0 0.1 select_select_fusion.2
  70.1 0.1 pad_maximum_fusion.u_ref
  70.2 27.0 %shard_map.37 = f32[2,5,32,8,128]{4,3,2,1,0:T(8,128)S(1)} custom-call(f32[1]{0:T(128)} %bitcast.5.ratio_ref, f32[2,5,40,8,128]{4,3,2,1,0:T(8,128)S(1)} %pad_maximum_fusion.u_ref, f32[2,5,32,8,128]{4,3,2,1,0:T(8,128)S(1)} %broadcast_select_fusion.base_ref), custom_call_target="tpu_custom_call" | custom-call | tf_op jit(solution)/shard_map/pallas_call | solution.py:215
  97.3 1.9 %collective-permute-start.3 = (f32[2,5,4,8,128]{4,3,2,1,0:T(8,128)S(1)}, f32[2,5,4,8,128]{4,3,2,1,0:T(8,128)S(1)}, u32[]{:S(2)}, u32[]{:S(2)}) collective-permute-start(f32[2,5,4,8,128]{4,3,2,1,0:T(8,128)S(1)} %get-tuple-element.12), channel_id=1, source_target_pairs={{0,1},{1,2},{2,3},{3,4},{4,5},{5,6},{6,7},{7,8},{8,9},{9,10},{10,1... | collective-permute-start | bytes 491528 | tf_op jit(solution)/shard_map/ppermute | solution.py:235
  99.2 2.4 %collective-permute-start.4 = (f32[2,5,4,8,128]{4,3,2,1,0:T(8,128)S(1)}, f32[2,5,4,8,128]{4,3,2,1,0:T(8,128)S(1)}, u32[]{:S(2)}, u32[]{:S(2)}) collective-permute-start(f32[2,5,4,8,128]{4,3,2,1,0:T(8,128)S(1)} %get-tuple-element.13), channel_id=1, source_target_pairs={{1,0},{2,1},{3,2},{4,3},{5,4},{6,5},{7,6},{8,7},{9,8},{10,9},{11,1... | collective-permute-start | bytes 491528 | tf_op jit(solution)/shard_map/ppermute | solution.py:236
  101.6 0.0 collective-permute-done.3
  101.6 0.6 gather_fusion.2
  102.2 0.1 select_select_fusion.1
  102.3 4.4 %collective-permute-done.4 = f32[2,5,4,8,128]{4,3,2,1,0:T(8,128)S(1)} collective-permute-done((f32[2,5,4,8,128]{4,3,2,1,0:T(8,128)S(1)}, f32[2,5,4,8,128]{4,3,2,1,0:T(8,128)S(1)}, u32[]{:S(2)}, u32[]{:S(2)}) %collective-permute-start.4) | collective-permute-done | bytes 163872 | tf_op jit(solution)/shard_map/ppermute | solution.py:236
  106.7 0.6 gather_fusion.3
  107.3 0.1 select_select_fusion
  107.4 0.1 pad_maximum_fusion.1.u_ref
  107.5 27.2 %shard_map.38 = f32[2,5,32,8,128]{4,3,2,1,0:T(8,128)S(1)} custom-call(f32[1]{0:T(128)} %bitcast.5.ratio_ref, f32[2,5,40,8,128]{4,3,2,1,0:T(8,128)S(1)} %pad_maximum_fusion.1.u_ref, f32[2,5,32,8,128]{4,3,2,1,0:T(8,128)S(1)} %broadcast_select_fusion.base_ref), custom_call_target="tpu_custom_call" | custom-call | tf_op jit(solution)/shard_map/pallas_call | solution.py:215
  134.7 1.3 reshape.51
  (10 shorter events, 0.1 us)
Async XLA Ops:
  2.2 3.4 %copy-start = (s32[2,3]{1,0:T(2,128)S(1)}, s32[2,3]{1,0:T(2,128)}, u32[]{:S(2)}) copy-start(s32[2,3]{1,0:T(2,128)} %param.7) | copy-start | bytes 76
  2.3 53.9 %collective-permute-start = (f32[5,32,8,128]{3,2,1,0:T(8,128)S(1)}, f32[5,32,8,128]{3,2,1,0:T(8,128)S(1)}, u32[]{:S(2)}, u32[]{:S(2)}) collective-permute-start(f32[5,32,8,128]{3,2,1,0:T(8,128)S(1)} %dynamic-slice_bitcast_fusion), channel_id=1, source_target_pairs={{0,16},{1,17},{2,18},{3,19},{4,20},{5,21},{6,22},{7,23},{8,24},{9,... | collective-permute-start | bytes 1966088 | tf_op jit(solution)/shard_map/ppermute | solution.py:252
  56.5 7.6 %collective-permute-start.1 = (f32[2,5,4,8,128]{4,3,2,1,0:T(8,128)S(1)}, f32[2,5,4,8,128]{4,3,2,1,0:T(8,128)S(1)}, u32[]{:S(2)}, u32[]{:S(2)}) collective-permute-start(f32[2,5,4,8,128]{4,3,2,1,0:T(8,128)S(1)} %get-tuple-element.16), channel_id=1, source_target_pairs={{0,1},{1,2},{2,3},{3,4},{4,5},{5,6},{6,7},{7,8},{8,9},{9,10},{10,1... | collective-permute-start | bytes 491528 | tf_op jit(solution)/shard_map/ppermute | solution.py:235
  61.9 7.5 %collective-permute-start.2 = (f32[2,5,4,8,128]{4,3,2,1,0:T(8,128)S(1)}, f32[2,5,4,8,128]{4,3,2,1,0:T(8,128)S(1)}, u32[]{:S(2)}, u32[]{:S(2)}) collective-permute-start(f32[2,5,4,8,128]{4,3,2,1,0:T(8,128)S(1)} %get-tuple-element.17), channel_id=1, source_target_pairs={{1,0},{2,1},{3,2},{4,3},{5,4},{6,5},{7,6},{8,7},{9,8},{10,9},{11,1... | collective-permute-start | bytes 491528 | tf_op jit(solution)/shard_map/ppermute | solution.py:236
  97.3 4.4 %collective-permute-start.3 = (f32[2,5,4,8,128]{4,3,2,1,0:T(8,128)S(1)}, f32[2,5,4,8,128]{4,3,2,1,0:T(8,128)S(1)}, u32[]{:S(2)}, u32[]{:S(2)}) collective-permute-start(f32[2,5,4,8,128]{4,3,2,1,0:T(8,128)S(1)} %get-tuple-element.12), channel_id=1, source_target_pairs={{0,1},{1,2},{2,3},{3,4},{4,5},{5,6},{6,7},{7,8},{8,9},{9,10},{10,1... | collective-permute-start | bytes 491528 | tf_op jit(solution)/shard_map/ppermute | solution.py:235
  99.2 7.5 %collective-permute-start.4 = (f32[2,5,4,8,128]{4,3,2,1,0:T(8,128)S(1)}, f32[2,5,4,8,128]{4,3,2,1,0:T(8,128)S(1)}, u32[]{:S(2)}, u32[]{:S(2)}) collective-permute-start(f32[2,5,4,8,128]{4,3,2,1,0:T(8,128)S(1)} %get-tuple-element.13), channel_id=1, source_target_pairs={{1,0},{2,1},{3,2},{4,3},{5,4},{6,5},{7,6},{8,7},{9,8},{10,9},{11,1... | collective-permute-start | bytes 491528 | tf_op jit(solution)/shard_map/ppermute | solution.py:236

commit v2 on v1

--- a/solution.py
+++ b/solution.py
@@ -135,23 +135,131 @@
     return [shift(x, 1) - x for x in flux]
 
 
-def rate_kernel(last, ratio_ref, u_ref, base_ref, out_ref, q_ref, t_ref, a_ref, chi_ref, up_ref, flux_ref):
+def step_kernel(
+    n, swap_ref, next_ref, cell_ref, out_ref,
+    u_ref, first_ref, q_ref, t_ref, a_ref, chi_ref, up_ref, flux_ref, ratio_ref,
+    sent_ref, came_ref, fast_ref, fast_in_ref, edge_ref, ghost_ref,
+    swap_send, swap_recv, fast_send, fast_recv, edge_send, edge_recv,
+):
     depth = out_ref.shape[2]
-    ratio = ratio_ref[0]
-
-    @pl.loop(0, depth + 2 * GHOST)
-    def _(e):
-        q = primitives([u_ref[:, f, e] for f in range(5)])
-        for f in range(5):
-            q_ref[f, e] = q[f]
+    chunks = depth // GHOST
+    rounds = n.bit_length() - 1
+    me = lax.axis_index("box")
+    right, left = lax.rem(me + 1, n), lax.rem(me + n - 1, n)
+    peers = [me + 2**k * (1 - 2 * lax.rem(lax.div(me, 2**k), 2)) for k in range(rounds)]
+    sent_slot = swap_ref[0]
+    kept_slot = 1 - sent_slot
+
+    barrier = pltpu.get_barrier_semaphore()
+    for peer in peers + [left, right]:
+        pl.semaphore_signal(barrier, inc=1, device_id=(peer,), device_id_type=pl.DeviceIdType.MESH)
+    pl.semaphore_wait(barrier, rounds + 2)
+
+    def remote(src, dst, send, recv, peer):
+        return pltpu.make_async_remote_copy(
+            src_ref=src, dst_ref=dst, send_sem=send, recv_sem=recv,
+            device_id=(peer,), device_id_type=pl.DeviceIdType.MESH,
+        )
+
+    def swap_copy(c):
+        part = pl.ds(c * GHOST, GHOST)
+        return remote(sent_ref.at[part], came_ref.at[part], swap_send.at[c], swap_recv.at[c], peers[-1])
+
+    def fast_copy(k):
+        return remote(fast_ref.at[k], fast_in_ref.at[k], fast_send.at[k], fast_recv.at[k], peers[k])
+
+    def edge_copy(stage, side):
+        i = 2 * stage + side
+        return remote(edge_ref.at[i], ghost_ref.at[i], edge_send.at[i], edge_recv.at[i], (left, right)[side])
+
+    @pl.loop(0, chunks)
+    def _(j):
+        c = lax.rem(j + chunks - 1, chunks)
+        for k in range(GHOST):
+            x = c * GHOST + k
+            for f in range(5):
+                sent_ref[x, f] = cell_ref[sent_slot, f, x]
+        swap_copy(c).start()
+
+    fast_ref[0] = jnp.zeros_like(fast_ref[0])
 
     @pl.loop(0, depth)
     def _(x):
-        q = [q_ref[f, x + GHOST] for f in range(5)]
+        speed = signal_speed(primitives([cell_ref[:, f, x] for f in range(5)]))
+        fast_ref[0] = jnp.maximum(fast_ref[0], jnp.maximum(speed[0], speed[1]))
+
+    def kept(pair):
+        x = 2 * pair
+        u = [cell_ref[kept_slot, f, pl.ds(x, 2)] for f in range(5)]
+        q = primitives(u)
+        dz = plane_sweep(q, z_shift, 3)
+        for f in range(5):
+            for k in range(2):
+                u_ref[f, x + k, 0] = u[f][k]
+                q_ref[f, x + GHOST + k, 0] = q[f][k]
+                t_ref[f, x + k, 0] = dz[f][k]
+
+    pairs = depth // 2
+    for k in range(rounds):
+        fast_copy(k).start()
+        pl.loop(pairs * k // rounds, pairs * (k + 1) // rounds)(kept)
+        fast_copy(k).wait()
+        fast_ref[k + 1] = jnp.maximum(fast_ref[k], fast_in_ref[k])
+    ratio_ref[...] = jnp.zeros_like(ratio_ref) + COURANT / jnp.max(fast_ref[rounds], keepdims=True)
+
+    def incoming(x):
+        u = [came_ref[x, f] for f in range(5)]
+        q = primitives(u)
+        for f in range(5):
+            u_ref[f, x, 1] = u[f]
+            q_ref[f, x + GHOST, 1] = q[f]
+        dz = plane_sweep([v[None] for v in q], z_shift, 3)
+        dy = plane_sweep([q_ref[f, x + GHOST] for f in range(5)], y_shift, 2)
+        for f in range(5):
+            t_ref[f, x] = dy[f] + jnp.concatenate([t_ref[f, x, 0][None], dz[f]], axis=0)
+
+    def both(x):
+        q = primitives([first_ref[f, x] for f in range(5)])
+        for f in range(5):
+            q_ref[f, x + GHOST] = q[f]
         dz = plane_sweep(q, z_shift, 3)
         dy = plane_sweep(q, y_shift, 2)
         for f in range(5):
             t_ref[f, x] = dz[f] + dy[f]
+
+    def by_slot(pair):
+        return jnp.where(sent_slot == 0, pair[1], pair[0]), jnp.where(sent_slot == 0, pair[0], pair[1])
+
+    def send_edge(stage, side, source_ref):
+        @pl.loop(0, GHOST)
+        def _(k):
+            for f in range(5):
+                zero, one = by_slot(source_ref[f, k + side * (depth - GHOST)])
+                edge_ref[2 * stage + side, 0, k, f] = zero
+                edge_ref[2 * stage + side, 1, k, f] = one
+
+        edge_copy(stage, side).start()
+
+    def take_ghosts(stage, side, source_ref):
+        edge_copy(stage, 1 - side).wait()
+        beside = [next_ref[slot, side] for slot in (kept_slot, sent_slot)]
+        base = (left, right)[side] * 2
+        own = side * (depth - 1)
+
+        @pl.loop(0, GHOST)
+        def _(k):
+            u = []
+            for f in range(5):
+                mine = source_ref[f, own]
+                parts = []
+                for role in range(2):
+                    zero, one = (ghost_ref[2 * stage + 1 - side, slot, k, f] for slot in range(2))
+                    theirs = jnp.where(beside[role] == base, zero, one)
+                    parts.append(jnp.where(beside[role] < 0, mine[role], theirs)[None])
+                u.append(jnp.concatenate(parts, axis=0))
+            q = primitives(u)
+            for f in range(5):
+                q_ref[f, k + side * (depth + GHOST)] = q[f]
 
     def chi_at(e):
         low, high = q_ref[4, e - 2], q_ref[4, e + 2]
@@ -175,16 +283,6 @@
             upper.append(high)
         return lower, upper
 
-    for f in range(5):
-        q = [q_ref[f, k] for k in (1, 2, 3, 4)]
-        d = q[2] - q[1]
-        a_ref[f] = d - face_offset(q[1] - q[0], d, q[3] - q[2])
-    chi_ref[0] = chi_at(2)
-    chi_ref[1] = chi_at(3)
-    _, upper = cell(3)
-    for f in range(5):
-        up_ref[f] = upper[f]
-
     def face(e):
         lower, upper = cell(e)
         flux = riemann([up_ref[f] for f in range(5)], lower, 1)
@@ -192,71 +290,110 @@
             up_ref[f] = upper[f]
         return flux
 
-    flux = face(GHOST)
-    for f in range(5):
-        flux_ref[f] = flux[f]
-
-    @pl.loop(0, depth)
-    def _(x):
+    def begin_x():
+        for f in range(5):
+            q = [q_ref[f, k] for k in (1, 2, 3, 4)]
+            d = q[2] - q[1]
+            a_ref[f] = d - face_offset(q[1] - q[0], d, q[3] - q[2])
+        chi_ref[0] = chi_at(2)
+        chi_ref[1] = chi_at(3)
+        _, upper = cell(3)
+        for f in range(5):
+            up_ref[f] = upper[f]
+        flux = face(GHOST)
+        for f in range(5):
+            flux_ref[f] = flux[f]
+
+    def rate_x(x):
         flux = face(x + GHOST + 1)
-        for f in range(5):
-            u = u_ref[:, f, x + GHOST]
-            new = u - ratio * (flux[f] - flux_ref[f] + t_ref[f, x])
-            if last:
-                new = 0.5 * (base_ref[:, f, x] + new)
-            out_ref[:, f, x] = new
+        rate = []
+        for f in range(5):
+            rate.append(ratio_ref[...] * (flux[f] - flux_ref[f] + t_ref[f, x]))
             flux_ref[f] = flux[f]
-
-
-def rate_step(last, ratio, extended, base):
-    slots, fields, depth = extended.shape[0], extended.shape[1], extended.shape[2] - 2 * GHOST
-    tile = (slots, 8, 128)
-    vmem = pl.BlockSpec(memory_space=pltpu.VMEM)
-    return pl.pallas_call(
-        functools.partial(rate_kernel, last),
-        out_shape=jax.ShapeDtypeStruct((slots, fields, depth, 8, 128), jnp.float32),
-        in_specs=[pl.BlockSpec(memory_space=pltpu.SMEM), vmem, vmem],
-        out_specs=vmem,
-        scratch_shapes=[
-            pltpu.VMEM((fields, depth + 2 * GHOST) + tile, jnp.float32),
-            pltpu.VMEM((fields, depth) + tile, jnp.float32),
-            pltpu.VMEM((fields,) + tile, jnp.float32),
-            pltpu.VMEM((2,) + tile, jnp.float32),
-            pltpu.VMEM((fields,) + tile, jnp.float32),
-            pltpu.VMEM((fields,) + tile, jnp.float32),
-        ],
-        compiler_params=pltpu.CompilerParams(vmem_limit_bytes=40 * 2**20),
-    )(ratio, extended, base)
-
-
-def extend(box_data, neighbours, own_start):
-    slots = box_data.shape[0]
-    count = lax.axis_size("box")
-    below = lax.ppermute(box_data[:, :, -GHOST:], "box", [(i, i + 1) for i in range(count - 1)])
-    above = lax.ppermute(box_data[:, :, :GHOST], "box", [(i + 1, i) for i in range(count - 1)])
-    lower, upper = neighbours[:, 0], neighbours[:, 1]
-    from_lower = jnp.take(below, jnp.clip(lower - own_start + slots, 0, slots - 1), axis=0)
-    from_upper = jnp.take(above, jnp.clip(upper - own_start - slots, 0, slots - 1), axis=0)
-    end = lambda x: (x < 0)[:, None, None, None, None]
-    low = jnp.where(end(lower), box_data[:, :, :1], from_lower)
-    high = jnp.where(end(upper), box_data[:, :, -1:], from_upper)
-    return jnp.concatenate([low, box_data, high], axis=2)
+        return rate
+
+    def first_x(x):
+        rate = rate_x(x)
+        for f in range(5):
+            first_ref[f, x] = u_ref[f, x] - rate[f]
+
+    def last_x(x):
+        rate = rate_x(x)
+        for f in range(5):
+            new = 0.5 * (u_ref[f, x] + (first_ref[f, x] - rate[f]))
+            zero, one = by_slot(new)
+            out_ref[0, f, x] = zero
+            out_ref[1, f, x] = one
+
+    swap_copy(chunks - 1).wait_recv()
+    swap_copy(0).wait_recv()
+    pl.loop(0, 2 * GHOST)(lambda j: incoming(lax.rem(j + depth - GHOST, depth)))
+    send_edge(0, 1, u_ref)
+    send_edge(0, 0, u_ref)
+
+    def middle(c):
+        swap_copy(c).wait_recv()
+        pl.loop(0, GHOST)(lambda k: incoming(c * GHOST + k))
+
+    middle(1)
+    take_ghosts(0, 0, u_ref)
+    begin_x()
+    pl.loop(0, GHOST)(first_x)
+
+    @pl.loop(2, chunks - 1)
+    def _(c):
+        middle(c)
+        pl.loop(0, GHOST)(lambda k: first_x(c * GHOST - GHOST + k))
+
+    take_ghosts(0, 1, u_ref)
+    pl.loop(depth - 2 * GHOST, depth)(first_x)
+    send_edge(1, 0, first_ref)
+    send_edge(1, 1, first_ref)
+    pl.loop(0, depth)(both)
+    take_ghosts(1, 0, first_ref)
+    take_ghosts(1, 1, first_ref)
+    begin_x()
+    pl.loop(0, depth)(last_x)
+    pl.loop(0, chunks)(lambda c: swap_copy(c).wait_send())
 
 
 def body(cell_state, swap_slots, neighbours):
     slots, fields, depth, _ = cell_state.shape
+    n = lax.axis_size("box")
+    rounds = n.bit_length() - 1
     cells = cell_state.reshape(slots, fields, depth, 8, 128)
-    chosen_slot = swap_slots[0]
-    count = lax.axis_size("box")
-    outgoing = lax.dynamic_index_in_dim(cells, chosen_slot, 0, keepdims=False)
-    incoming = lax.ppermute(outgoing, "box", [(i, i ^ (count // 2)) for i in range(count)])
-    fast = jnp.max(signal_speed(primitives([cells[:, f] for f in range(fields)])))
-    ratio = (COURANT / lax.pmax(fast, "box")).reshape(1)
-    chosen = jnp.arange(slots, dtype=jnp.int32) == chosen_slot
-    box_data = jnp.where(chosen[:, None, None, None, None], incoming[None], cells)
-    own_start = lax.axis_index("box") * slots
-    first = rate_step(False, ratio, extend(box_data, neighbours, own_start), box_data)
-    new = rate_step(True, ratio, extend(first, neighbours, own_start), box_data)
+    vmem, smem = (pl.BlockSpec(memory_space=space) for space in (pltpu.VMEM, pltpu.SMEM))
+    pair = (slots, 8, 128)
+    tile = (8, 128)
+    scratch = [
+        (fields, depth) + pair,
+        (fields, depth) + pair,
+        (fields, depth + 2 * GHOST) + pair,
+        (fields, depth) + pair,
+        (fields,) + pair,
+        (2,) + pair,
+        (fields,) + pair,
+        (fields,) + pair,
+        tile,
+        (depth, fields) + tile,
+        (depth, fields) + tile,
+        (rounds + 1,) + tile,
+        (rounds,) + tile,
+        (4, slots, GHOST, fields) + tile,
+        (4, slots, GHOST, fields) + tile,
+    ]
+    counts = [depth // GHOST] * 2 + [rounds] * 2 + [4] * 2
+    new = pl.pallas_call(
+        functools.partial(step_kernel, n),
+        out_shape=jax.ShapeDtypeStruct(cells.shape, jnp.float32),
+        in_specs=[smem, smem, vmem],
+        out_specs=vmem,
+        scratch_shapes=[pltpu.VMEM(s, jnp.float32) for s in scratch]
+        + [pltpu.SemaphoreType.DMA((k,)) for k in counts],
+        compiler_params=pltpu.CompilerParams(
+            vmem_limit_bytes=40 * 2**20, collective_id=0, has_side_effects=True
+        ),
+    )(swap_slots, neighbours, cells)
     return new.reshape(cell_state.shape)
 
 

time: 136 us -> 95.6 us (0.70)
  the two profiles are of different devices: /device:TPU:3 before, /device:TPU:0 now
where the time goes in v2:
time: 95.6 us; the launch traced here: 95.5 us
  Pallas kernels  92 us (96%)
  local copies, waits for them, and re-layouts  2.85 us (3%)
    pallas_call x1, Pallas kernels, body(): pl.pallas_call(functools.partial(step_kernel, n), out_shape=jax.ShapeDtyp...  92 us

profile of v2, /device:TPU:0, one launch (start us, length us, event | category | flops | bytes accessed | tf_op | source)
XLA Modules:
  0.0 95.5 jit_solution(5281894324625590190)
XLA Ops:
  0.7 0.0 copy-start
  0.7 1.6 %copy.4 = f32[40,8,8,128]{3,2,1,0:T(8,128)S(1)} copy(f32[40,8,8,128]{3,1,2,0:T(8,128)} %bitcast.8) | data formatting | bytes 2621440
  2.3 0.0 copy-done
  2.3 92.0 %shard_map.37 = f32[2,5,32,8,128]{4,3,2,1,0:T(8,128)S(1)} custom-call(s32[1]{0:T(128)S(6)} %copy.5.swap_ref, s32[2,3]{1,0:T(2,128)S(1)} %copy-done, f32[2,5,32,8,128]{4,3,2,1,0:T(8,128)S(1)} %bitcast.7), custom_call_target="tpu_custom_call" | custom-call | tf_op jit(solution)/shard_map/pallas_call | solution.py:386
  94.2 1.3 %reshape.7 = f32[2,5,32,1024]{3,2,1,0:T(8,128)} reshape(f32[2,5,32,8,128]{4,3,2,1,0:T(8,128)S(1)} %shard_map.37) | data formatting | bytes 2621440 | tf_op jit(solution)/shard_map/reshape | solution.py:397
Async XLA Ops:
  0.7 1.6 %copy-start = (s32[2,3]{1,0:T(2,128)S(1)}, s32[2,3]{1,0:T(2,128)}, u32[]{:S(2)}) copy-start(s32[2,3]{1,0:T(2,128)} %next_ref.1) | copy-start | bytes 76

commit v3 on v2

--- a/solution.py
+++ b/solution.py
@@ -11,6 +11,7 @@
 GHOST = 4
 RIEMANN_ITERS = 3
 COURANT = 0.4
+XSTEP = 2
 
 
 def rcp(x):
@@ -114,7 +115,7 @@
     row = lax.broadcasted_iota(jnp.int32, x.shape, 1)
     turned = pltpu.roll(x, (-n * BZC) % 128, 2)
     moved = pltpu.roll(turned, 7 if n > 0 else 1, 1)
-    other = jnp.concatenate([moved[1:], moved[:1]], axis=0)
+    other = jnp.concatenate([moved[i ^ 1][None] for i in range(x.shape[0])], axis=0)
     carry = jnp.where(row == (7 if n > 0 else 0), other, moved)
     keep = lane < 128 - n * BZC if n > 0 else lane >= -n * BZC
     return jnp.where(keep, turned, carry)
@@ -183,49 +184,56 @@
 
     fast_ref[0] = jnp.zeros_like(fast_ref[0])
 
-    @pl.loop(0, depth)
-    def _(x):
-        speed = signal_speed(primitives([cell_ref[:, f, x] for f in range(5)]))
-        fast_ref[0] = jnp.maximum(fast_ref[0], jnp.maximum(speed[0], speed[1]))
-
-    def kept(pair):
-        x = 2 * pair
-        u = [cell_ref[kept_slot, f, pl.ds(x, 2)] for f in range(5)]
+    @pl.loop(0, chunks)
+    def _(c):
+        speed = signal_speed(primitives([cell_ref[:, f, pl.ds(c * GHOST, GHOST)] for f in range(5)]))
+        fast_ref[0] = jnp.maximum(fast_ref[0], jnp.max(speed, axis=(0, 1)))
+
+    def kept(c):
+        x = c * GHOST
+        u = [cell_ref[kept_slot, f, pl.ds(x, GHOST)] for f in range(5)]
         q = primitives(u)
         dz = plane_sweep(q, z_shift, 3)
         for f in range(5):
-            for k in range(2):
+            for k in range(GHOST):
                 u_ref[f, x + k, 0] = u[f][k]
                 q_ref[f, x + GHOST + k, 0] = q[f][k]
                 t_ref[f, x + k, 0] = dz[f][k]
 
-    pairs = depth // 2
     for k in range(rounds):
         fast_copy(k).start()
-        pl.loop(pairs * k // rounds, pairs * (k + 1) // rounds)(kept)
+        pl.loop(chunks * k // rounds, chunks * (k + 1) // rounds)(kept)
         fast_copy(k).wait()
         fast_ref[k + 1] = jnp.maximum(fast_ref[k], fast_in_ref[k])
     ratio_ref[...] = jnp.zeros_like(ratio_ref) + COURANT / jnp.max(fast_ref[rounds], keepdims=True)
 
+    def planes(ref, f, x, m):
+        return ref[f, pl.ds(x, m)].reshape(2 * m, 8, 128)
+
+    def put(ref, f, x, m, value):
+        ref[f, pl.ds(x, m)] = value.reshape(m, 2, 8, 128)
+
     def incoming(x):
-        u = [came_ref[x, f] for f in range(5)]
+        u = [came_ref[pl.ds(x, 2), f] for f in range(5)]
         q = primitives(u)
         for f in range(5):
-            u_ref[f, x, 1] = u[f]
-            q_ref[f, x + GHOST, 1] = q[f]
-        dz = plane_sweep([v[None] for v in q], z_shift, 3)
-        dy = plane_sweep([q_ref[f, x + GHOST] for f in range(5)], y_shift, 2)
-        for f in range(5):
-            t_ref[f, x] = dy[f] + jnp.concatenate([t_ref[f, x, 0][None], dz[f]], axis=0)
+            for k in range(2):
+                u_ref[f, x + k, 1] = u[f][k]
+                q_ref[f, x + GHOST + k, 1] = q[f][k]
+        dz = plane_sweep(q, z_shift, 3)
+        dy = plane_sweep([planes(q_ref, f, x + GHOST, 2) for f in range(5)], y_shift, 2)
+        for f in range(5):
+            along_z = [part[None] for k in range(2) for part in (t_ref[f, x + k, 0], dz[f][k])]
+            put(t_ref, f, x, 2, dy[f] + jnp.concatenate(along_z, axis=0))
 
     def both(x):
-        q = primitives([first_ref[f, x] for f in range(5)])
-        for f in range(5):
-            q_ref[f, x + GHOST] = q[f]
+        q = primitives([planes(first_ref, f, x, 2) for f in range(5)])
+        for f in range(5):
+            put(q_ref, f, x + GHOST, 2, q[f])
         dz = plane_sweep(q, z_shift, 3)
         dy = plane_sweep(q, y_shift, 2)
         for f in range(5):
-            t_ref[f, x] = dz[f] + dy[f]
+            put(t_ref, f, x, 2, dz[f] + dy[f])
 
     def by_slot(pair):
         return jnp.where(sent_slot == 0, pair[1], pair[0]), jnp.where(sent_slot == 0, pair[0], pair[1])
@@ -261,33 +269,36 @@
             for f in range(5):
                 q_ref[f, k + side * (depth + GHOST)] = q[f]
 
-    def chi_at(e):
-        low, high = q_ref[4, e - 2], q_ref[4, e + 2]
-        return shock(
-            q_ref[4, e + 1] - q_ref[4, e - 1], high - low, high + low, q_ref[1, e - 1] - q_ref[1, e + 1]
-        )
-
-    def cell(e):
-        chi_next = chi_at(e + 1)
-        flat = 1.0 - jnp.maximum(jnp.maximum(chi_ref[0], chi_ref[1]), chi_next)
-        chi_ref[0] = chi_ref[1]
-        chi_ref[1] = chi_next
+    def chi_at(e, m):
+        p = [planes(q_ref, 4, e + k, m) for k in (-2, -1, 1, 2)]
+        v = [planes(q_ref, 1, e + k, m) for k in (-1, 1)]
+        return shock(p[2] - p[1], p[3] - p[0], p[3] + p[0], v[0] - v[1])
+
+    def shifted(first, rest):
+        return first if rest.shape[0] == 2 else jnp.concatenate([first, rest[:-2]], axis=0)
+
+    def cell(e, m):
+        chi = jnp.concatenate([chi_ref[0], chi_ref[1], chi_at(e + 1, m)], axis=0)
+        flat = 1.0 - jnp.maximum(jnp.maximum(chi[:-4], chi[2:-2]), chi[4:])
+        chi_ref[0] = chi[-4:-2]
+        chi_ref[1] = chi[-2:]
         lower, upper = [], []
         for f in range(5):
-            q = [q_ref[f, e + k] for k in (-1, 0, 1, 2)]
+            q = [planes(q_ref, f, e + k, m) for k in (-1, 0, 1, 2)]
             d = q[2] - q[1]
             b = face_offset(q[1] - q[0], d, q[3] - q[2])
-            low, high = edges(q[1], a_ref[f], b, flat)
-            a_ref[f] = d - b
+            a = d - b
+            low, high = edges(q[1], shifted(a_ref[f], a), b, flat)
+            a_ref[f] = a[-2:]
             lower.append(low)
             upper.append(high)
         return lower, upper
 
-    def face(e):
-        lower, upper = cell(e)
-        flux = riemann([up_ref[f] for f in range(5)], lower, 1)
-        for f in range(5):
-            up_ref[f] = upper[f]
+    def face(e, m):
+        lower, upper = cell(e, m)
+        flux = riemann([shifted(up_ref[f], upper[f]) for f in range(5)], lower, 1)
+        for f in range(5):
+            up_ref[f] = upper[f][-2:]
         return flux
 
     def begin_x():
@@ -295,65 +306,67 @@
             q = [q_ref[f, k] for k in (1, 2, 3, 4)]
             d = q[2] - q[1]
             a_ref[f] = d - face_offset(q[1] - q[0], d, q[3] - q[2])
-        chi_ref[0] = chi_at(2)
-        chi_ref[1] = chi_at(3)
-        _, upper = cell(3)
+        chi_ref[0] = chi_at(2, 1)
+        chi_ref[1] = chi_at(3, 1)
+        _, upper = cell(3, 1)
         for f in range(5):
             up_ref[f] = upper[f]
-        flux = face(GHOST)
+        flux = face(GHOST, 1)
         for f in range(5):
             flux_ref[f] = flux[f]
 
     def rate_x(x):
-        flux = face(x + GHOST + 1)
+        flux = face(x + GHOST + 1, XSTEP)
         rate = []
         for f in range(5):
-            rate.append(ratio_ref[...] * (flux[f] - flux_ref[f] + t_ref[f, x]))
-            flux_ref[f] = flux[f]
+            change = flux[f] - shifted(flux_ref[f], flux[f]) + planes(t_ref, f, x, XSTEP)
+            rate.append(ratio_ref[...] * change)
+            flux_ref[f] = flux[f][-2:]
         return rate
 
     def first_x(x):
         rate = rate_x(x)
         for f in range(5):
-            first_ref[f, x] = u_ref[f, x] - rate[f]
+            put(first_ref, f, x, XSTEP, planes(u_ref, f, x, XSTEP) - rate[f])
 
     def last_x(x):
         rate = rate_x(x)
         for f in range(5):
-            new = 0.5 * (u_ref[f, x] + (first_ref[f, x] - rate[f]))
-            zero, one = by_slot(new)
-            out_ref[0, f, x] = zero
-            out_ref[1, f, x] = one
+            new = 0.5 * (planes(u_ref, f, x, XSTEP) + (planes(first_ref, f, x, XSTEP) - rate[f]))
+            for k in range(XSTEP):
+                zero, one = by_slot(new[2 * k : 2 * k + 2])
+                out_ref[0, f, x + k] = zero
+                out_ref[1, f, x + k] = one
 
     swap_copy(chunks - 1).wait_recv()
     swap_copy(0).wait_recv()
-    pl.loop(0, 2 * GHOST)(lambda j: incoming(lax.rem(j + depth - GHOST, depth)))
+    pl.loop(0, GHOST)(lambda j: incoming(lax.rem(2 * j + depth - GHOST, depth)))
     send_edge(0, 1, u_ref)
     send_edge(0, 0, u_ref)
 
     def middle(c):
         swap_copy(c).wait_recv()
-        pl.loop(0, GHOST)(lambda k: incoming(c * GHOST + k))
+        pl.loop(0, GHOST // 2)(lambda k: incoming(c * GHOST + 2 * k))
 
     middle(1)
     take_ghosts(0, 0, u_ref)
     begin_x()
-    pl.loop(0, GHOST)(first_x)
+    pl.loop(0, GHOST, step=XSTEP)(first_x)
 
     @pl.loop(2, chunks - 1)
     def _(c):
         middle(c)
-        pl.loop(0, GHOST)(lambda k: first_x(c * GHOST - GHOST + k))
+        pl.loop(0, GHOST, step=XSTEP)(lambda k: first_x(c * GHOST - GHOST + k))
 
     take_ghosts(0, 1, u_ref)
-    pl.loop(depth - 2 * GHOST, depth)(first_x)
+    pl.loop(depth - 2 * GHOST, depth, step=XSTEP)(first_x)
     send_edge(1, 0, first_ref)
     send_edge(1, 1, first_ref)
-    pl.loop(0, depth)(both)
+    pl.loop(0, depth, step=2)(both)
     take_ghosts(1, 0, first_ref)
     take_ghosts(1, 1, first_ref)
     begin_x()
-    pl.loop(0, depth)(last_x)
+    pl.loop(0, depth, step=XSTEP)(last_x)
     pl.loop(0, chunks)(lambda c: swap_copy(c).wait_send())
 
 

time: 95.6 us -> 79.7 us (0.83)
  Pallas kernels: 92 us -> 76 us
    pallas_call x1, Pallas kernels: 92 us -> 76 us  [body(): pl.pallas_call(functools.partial(step_kernel, n), out_shape=jax.ShapeDtyp...]
where the time goes in v3:
time: 79.7 us; the launch traced here: 79.5 us
  Pallas kernels  76 us (95%)
  local copies, waits for them, and re-layouts  2.85 us (4%)
    pallas_call x1, Pallas kernels, body(): pl.pallas_call(functools.partial(step_kernel, n), out_shape=jax.ShapeDtyp...  76 us

profile of v3, /device:TPU:0, one launch (start us, length us, event | category | flops | bytes accessed | tf_op | source)
XLA Modules:
  0.0 79.5 jit_solution(9330050146693772616)
XLA Ops:
  0.7 0.0 copy-start
  0.7 1.6 %copy.4 = f32[40,8,8,128]{3,2,1,0:T(8,128)S(1)} copy(f32[40,8,8,128]{3,1,2,0:T(8,128)} %bitcast.8) | data formatting | bytes 2621440
  2.3 0.0 copy-done
  2.3 76.0 %shard_map.37 = f32[2,5,32,8,128]{4,3,2,1,0:T(8,128)S(1)} custom-call(s32[1]{0:T(128)S(6)} %copy.5.swap_ref, s32[2,3]{1,0:T(2,128)S(1)} %copy-done, f32[2,5,32,8,128]{4,3,2,1,0:T(8,128)S(1)} %bitcast.7), custom_call_target="tpu_custom_call" | custom-call | tf_op jit(solution)/shard_map/pallas_call | solution.py:399
  78.3 1.3 %reshape.7 = f32[2,5,32,1024]{3,2,1,0:T(8,128)} reshape(f32[2,5,32,8,128]{4,3,2,1,0:T(8,128)S(1)} %shard_map.37) | data formatting | bytes 2621440 | tf_op jit(solution)/shard_map/reshape | solution.py:410
Async XLA Ops:
  0.7 1.6 %copy-start = (s32[2,3]{1,0:T(2,128)S(1)}, s32[2,3]{1,0:T(2,128)}, u32[]{:S(2)}) copy-start(s32[2,3]{1,0:T(2,128)} %next_ref.1) | copy-start | bytes 76

commit v4 on v3

--- a/solution.py
+++ b/solution.py
@@ -12,6 +12,7 @@
 RIEMANN_ITERS = 3
 COURANT = 0.4
 XSTEP = 2
+IN_FLIGHT = 3
 
 
 def rcp(x):
@@ -173,15 +174,25 @@
         i = 2 * stage + side
         return remote(edge_ref.at[i], ghost_ref.at[i], edge_send.at[i], edge_recv.at[i], (left, right)[side])
 
-    @pl.loop(0, chunks)
-    def _(j):
-        c = lax.rem(j + chunks - 1, chunks)
+    def chunk(j):
+        return lax.rem(j + chunks - 1, chunks)
+
+    def launch(j):
+        c = chunk(j)
         for k in range(GHOST):
             x = c * GHOST + k
             for f in range(5):
                 sent_ref[x, f] = cell_ref[sent_slot, f, x]
         swap_copy(c).start()
 
+    def arrive(j):
+        swap_copy(chunk(j)).wait()
+
+        @pl.when(j + IN_FLIGHT < chunks)
+        def _():
+            launch(j + IN_FLIGHT)
+
+    pl.loop(0, IN_FLIGHT)(launch)
     fast_ref[0] = jnp.zeros_like(fast_ref[0])
 
     @pl.loop(0, chunks)
@@ -338,14 +349,14 @@
                 out_ref[0, f, x + k] = zero
                 out_ref[1, f, x + k] = one
 
-    swap_copy(chunks - 1).wait_recv()
-    swap_copy(0).wait_recv()
+    arrive(0)
+    arrive(1)
     pl.loop(0, GHOST)(lambda j: incoming(lax.rem(2 * j + depth - GHOST, depth)))
     send_edge(0, 1, u_ref)
     send_edge(0, 0, u_ref)
 
     def middle(c):
-        swap_copy(c).wait_recv()
+        arrive(c + 1)
         pl.loop(0, GHOST // 2)(lambda k: incoming(c * GHOST + 2 * k))
 
     middle(1)
@@ -367,7 +378,6 @@
     take_ghosts(1, 1, first_ref)
     begin_x()
     pl.loop(0, depth, step=XSTEP)(last_x)
-    pl.loop(0, chunks)(lambda c: swap_copy(c).wait_send())
 
 
 def body(cell_state, swap_slots, neighbours):

time: 79.7 us -> 65.9 us (0.83)
  Pallas kernels: 76 us -> 62.2 us
    pallas_call x1, Pallas kernels: 76 us -> 62.2 us  [body(): pl.pallas_call(functools.partial(step_kernel, n), out_shape=jax.ShapeDtyp...]
where the time goes in v4:
time: 65.9 us; the launch traced here: 65.8 us
  Pallas kernels  62.2 us (94%)
  local copies, waits for them, and re-layouts  2.85 us (4%)
  between operations  0.68 us (1%)
    pallas_call x1, Pallas kernels, body(): pl.pallas_call(functools.partial(step_kernel, n), out_shape=jax.ShapeDtyp...  62.2 us
    unnamed x3, local copies, waits for them, and re-layouts  1.59 us

profile of v4, /device:TPU:0, one launch (start us, length us, event | category | flops | bytes accessed | tf_op | source)
XLA Modules:
  0.0 65.8 jit_solution(15838632647393373383)
XLA Ops:
  0.7 0.0 copy-start
  0.7 1.6 %copy.4 = f32[40,8,8,128]{3,2,1,0:T(8,128)S(1)} copy(f32[40,8,8,128]{3,1,2,0:T(8,128)} %bitcast.8) | data formatting | bytes 2621440
  2.3 0.0 copy-done
  2.3 62.2 %shard_map.37 = f32[2,5,32,8,128]{4,3,2,1,0:T(8,128)S(1)} custom-call(s32[1]{0:T(128)S(6)} %copy.5.swap_ref, s32[2,3]{1,0:T(2,128)S(1)} %copy-done, f32[2,5,32,8,128]{4,3,2,1,0:T(8,128)S(1)} %bitcast.7), custom_call_target="tpu_custom_call" | custom-call | tf_op jit(solution)/shard_map/pallas_call | solution.py:409
  64.5 1.3 %reshape.7 = f32[2,5,32,1024]{3,2,1,0:T(8,128)} reshape(f32[2,5,32,8,128]{4,3,2,1,0:T(8,128)S(1)} %shard_map.37) | data formatting | bytes 2621440 | tf_op jit(solution)/shard_map/reshape | solution.py:420
Async XLA Ops:
  0.7 1.6 %copy-start = (s32[2,3]{1,0:T(2,128)S(1)}, s32[2,3]{1,0:T(2,128)}, u32[]{:S(2)}) copy-start(s32[2,3]{1,0:T(2,128)} %next_ref.1) | copy-start | bytes 76

commit v5 on v4

--- a/solution.py
+++ b/solution.py
@@ -13,6 +13,7 @@
 COURANT = 0.4
 XSTEP = 2
 IN_FLIGHT = 3
+LEAD = 8
 
 
 def rcp(x):
@@ -237,10 +238,14 @@
             along_z = [part[None] for k in range(2) for part in (t_ref[f, x + k, 0], dz[f][k])]
             put(t_ref, f, x, 2, dy[f] + jnp.concatenate(along_z, axis=0))
 
+    def prims(c):
+        x = c * GHOST
+        q = primitives([planes(first_ref, f, x, GHOST) for f in range(5)])
+        for f in range(5):
+            put(q_ref, f, x + GHOST, GHOST, q[f])
+
     def both(x):
-        q = primitives([planes(first_ref, f, x, 2) for f in range(5)])
-        for f in range(5):
-            put(q_ref, f, x + GHOST, 2, q[f])
+        q = [planes(q_ref, f, x + GHOST, 2) for f in range(5)]
         dz = plane_sweep(q, z_shift, 3)
         dy = plane_sweep(q, y_shift, 2)
         for f in range(5):
@@ -373,11 +378,18 @@
     pl.loop(depth - 2 * GHOST, depth, step=XSTEP)(first_x)
     send_edge(1, 0, first_ref)
     send_edge(1, 1, first_ref)
-    pl.loop(0, depth, step=2)(both)
+    pl.loop(0, chunks)(prims)
+    pl.loop(0, LEAD, step=2)(both)
     take_ghosts(1, 0, first_ref)
     take_ghosts(1, 1, first_ref)
     begin_x()
-    pl.loop(0, depth, step=XSTEP)(last_x)
+
+    @pl.loop(0, depth - LEAD, step=2)
+    def _(x):
+        last_x(x)
+        both(x + LEAD)
+
+    pl.loop(depth - LEAD, depth, step=XSTEP)(last_x)
 
 
 def body(cell_state, swap_slots, neighbours):

time: 65.9 us -> 64.8 us (0.983)
  Pallas kernels: 62.2 us -> 61.2 us
    pallas_call x1, Pallas kernels: 62.2 us -> 61.2 us  [body(): pl.pallas_call(functools.partial(step_kernel, n), out_shape=jax.ShapeDtyp...]
where the time goes in v5:
time: 64.8 us; the launch traced here: 64.7 us
  Pallas kernels  61.2 us (94%)
  local copies, waits for them, and re-layouts  2.85 us (4%)
  between operations  0.68 us (1%)
    pallas_call x1, Pallas kernels, body(): pl.pallas_call(functools.partial(step_kernel, n), out_shape=jax.ShapeDtyp...  61.2 us
    unnamed x3, local copies, waits for them, and re-layouts  1.59 us

profile of v5, /device:TPU:0, one launch (start us, length us, event | category | flops | bytes accessed | tf_op | source)
XLA Modules:
  0.0 64.7 jit_solution(16054579674291467306)
XLA Ops:
  0.7 0.0 copy-start
  0.7 1.6 %copy.4 = f32[40,8,8,128]{3,2,1,0:T(8,128)S(1)} copy(f32[40,8,8,128]{3,1,2,0:T(8,128)} %bitcast.8) | data formatting | bytes 2621440
  2.3 0.0 copy-done
  2.3 61.2 %shard_map.37 = f32[2,5,32,8,128]{4,3,2,1,0:T(8,128)S(1)} custom-call(s32[1]{0:T(128)S(6)} %copy.5.swap_ref, s32[2,3]{1,0:T(2,128)S(1)} %copy-done, f32[2,5,32,8,128]{4,3,2,1,0:T(8,128)S(1)} %bitcast.7), custom_call_target="tpu_custom_call" | custom-call | tf_op jit(solution)/shard_map/pallas_call | solution.py:421
  63.4 1.3 %reshape.7 = f32[2,5,32,1024]{3,2,1,0:T(8,128)} reshape(f32[2,5,32,8,128]{4,3,2,1,0:T(8,128)S(1)} %shard_map.37) | data formatting | bytes 2621440 | tf_op jit(solution)/shard_map/reshape | solution.py:432
Async XLA Ops:
  0.7 1.6 %copy-start = (s32[2,3]{1,0:T(2,128)S(1)}, s32[2,3]{1,0:T(2,128)}, u32[]{:S(2)}) copy-start(s32[2,3]{1,0:T(2,128)} %next_ref.1) | copy-start | bytes 76

commit v6 on v4

--- a/solution.py
+++ b/solution.py
@@ -13,6 +13,7 @@
 COURANT = 0.4
 XSTEP = 2
 IN_FLIGHT = 3
+LAST_XSTEP = 4
 
 
 def rcp(x):
@@ -139,7 +140,7 @@
 
 def step_kernel(
     n, swap_ref, next_ref, cell_ref, out_ref,
-    u_ref, first_ref, q_ref, t_ref, a_ref, chi_ref, up_ref, flux_ref, ratio_ref,
+    u_ref, first_ref, q_ref, t_ref, q_two_ref, t_two_ref, a_ref, chi_ref, up_ref, flux_ref, ratio_ref,
     sent_ref, came_ref, fast_ref, fast_in_ref, edge_ref, ghost_ref,
     swap_send, swap_recv, fast_send, fast_recv, edge_send, edge_recv,
 ):
@@ -237,14 +238,14 @@
             along_z = [part[None] for k in range(2) for part in (t_ref[f, x + k, 0], dz[f][k])]
             put(t_ref, f, x, 2, dy[f] + jnp.concatenate(along_z, axis=0))
 
-    def both(x):
+    def second(x):
         q = primitives([planes(first_ref, f, x, 2) for f in range(5)])
         for f in range(5):
-            put(q_ref, f, x + GHOST, 2, q[f])
+            put(q_two_ref, f, x + GHOST, 2, q[f])
         dz = plane_sweep(q, z_shift, 3)
         dy = plane_sweep(q, y_shift, 2)
         for f in range(5):
-            put(t_ref, f, x, 2, dz[f] + dy[f])
+            put(t_two_ref, f, x, 2, dz[f] + dy[f])
 
     def by_slot(pair):
         return jnp.where(sent_slot == 0, pair[1], pair[0]), jnp.where(sent_slot == 0, pair[0], pair[1])
@@ -258,6 +259,8 @@
                 edge_ref[2 * stage + side, 1, k, f] = one
 
         edge_copy(stage, side).start()
+
+    prim_refs = (q_ref, q_two_ref)
 
     def take_ghosts(stage, side, source_ref):
         edge_copy(stage, 1 - side).wait()
@@ -278,24 +281,24 @@
                 u.append(jnp.concatenate(parts, axis=0))
             q = primitives(u)
             for f in range(5):
-                q_ref[f, k + side * (depth + GHOST)] = q[f]
-
-    def chi_at(e, m):
-        p = [planes(q_ref, 4, e + k, m) for k in (-2, -1, 1, 2)]
-        v = [planes(q_ref, 1, e + k, m) for k in (-1, 1)]
+                prim_refs[stage][f, k + side * (depth + GHOST)] = q[f]
+
+    def chi_at(prim_ref, e, m):
+        p = [planes(prim_ref, 4, e + k, m) for k in (-2, -1, 1, 2)]
+        v = [planes(prim_ref, 1, e + k, m) for k in (-1, 1)]
         return shock(p[2] - p[1], p[3] - p[0], p[3] + p[0], v[0] - v[1])
 
     def shifted(first, rest):
         return first if rest.shape[0] == 2 else jnp.concatenate([first, rest[:-2]], axis=0)
 
-    def cell(e, m):
-        chi = jnp.concatenate([chi_ref[0], chi_ref[1], chi_at(e + 1, m)], axis=0)
+    def cell(prim_ref, e, m):
+        chi = jnp.concatenate([chi_ref[0], chi_ref[1], chi_at(prim_ref, e + 1, m)], axis=0)
         flat = 1.0 - jnp.maximum(jnp.maximum(chi[:-4], chi[2:-2]), chi[4:])
         chi_ref[0] = chi[-4:-2]
         chi_ref[1] = chi[-2:]
         lower, upper = [], []
         for f in range(5):
-            q = [planes(q_ref, f, e + k, m) for k in (-1, 0, 1, 2)]
+            q = [planes(prim_ref, f, e + k, m) for k in (-1, 0, 1, 2)]
             d = q[2] - q[1]
             b = face_offset(q[1] - q[0], d, q[3] - q[2])
             a = d - b
@@ -305,46 +308,46 @@
             upper.append(high)
         return lower, upper
 
-    def face(e, m):
-        lower, upper = cell(e, m)
+    def face(prim_ref, e, m):
+        lower, upper = cell(prim_ref, e, m)
         flux = riemann([shifted(up_ref[f], upper[f]) for f in range(5)], lower, 1)
         for f in range(5):
             up_ref[f] = upper[f][-2:]
         return flux
 
-    def begin_x():
-        for f in range(5):
-            q = [q_ref[f, k] for k in (1, 2, 3, 4)]
+    def begin_x(prim_ref):
+        for f in range(5):
+            q = [prim_ref[f, k] for k in (1, 2, 3, 4)]
             d = q[2] - q[1]
             a_ref[f] = d - face_offset(q[1] - q[0], d, q[3] - q[2])
-        chi_ref[0] = chi_at(2, 1)
-        chi_ref[1] = chi_at(3, 1)
-        _, upper = cell(3, 1)
+        chi_ref[0] = chi_at(prim_ref, 2, 1)
+        chi_ref[1] = chi_at(prim_ref, 3, 1)
+        _, upper = cell(prim_ref, 3, 1)
         for f in range(5):
             up_ref[f] = upper[f]
-        flux = face(GHOST, 1)
+        flux = face(prim_ref, GHOST, 1)
         for f in range(5):
             flux_ref[f] = flux[f]
 
-    def rate_x(x):
-        flux = face(x + GHOST + 1, XSTEP)
+    def rate_x(prim_ref, rest_ref, x, m):
+        flux = face(prim_ref, x + GHOST + 1, m)
         rate = []
         for f in range(5):
-            change = flux[f] - shifted(flux_ref[f], flux[f]) + planes(t_ref, f, x, XSTEP)
+            change = flux[f] - shifted(flux_ref[f], flux[f]) + planes(rest_ref, f, x, m)
             rate.append(ratio_ref[...] * change)
             flux_ref[f] = flux[f][-2:]
         return rate
 
     def first_x(x):
-        rate = rate_x(x)
+        rate = rate_x(q_ref, t_ref, x, XSTEP)
         for f in range(5):
             put(first_ref, f, x, XSTEP, planes(u_ref, f, x, XSTEP) - rate[f])
 
     def last_x(x):
-        rate = rate_x(x)
-        for f in range(5):
-            new = 0.5 * (planes(u_ref, f, x, XSTEP) + (planes(first_ref, f, x, XSTEP) - rate[f]))
-            for k in range(XSTEP):
+        rate = rate_x(q_two_ref, t_two_ref, x, LAST_XSTEP)
+        for f in range(5):
+            new = 0.5 * (planes(u_ref, f, x, LAST_XSTEP) + (planes(first_ref, f, x, LAST_XSTEP) - rate[f]))
+            for k in range(LAST_XSTEP):
                 zero, one = by_slot(new[2 * k : 2 * k + 2])
                 out_ref[0, f, x + k] = zero
                 out_ref[1, f, x + k] = one
@@ -361,23 +364,27 @@
 
     middle(1)
     take_ghosts(0, 0, u_ref)
-    begin_x()
+    begin_x(q_ref)
     pl.loop(0, GHOST, step=XSTEP)(first_x)
 
     @pl.loop(2, chunks - 1)
     def _(c):
         middle(c)
-        pl.loop(0, GHOST, step=XSTEP)(lambda k: first_x(c * GHOST - GHOST + k))
-
+
+        @pl.loop(c * GHOST - GHOST, c * GHOST, step=XSTEP)
+        def _(x):
+            first_x(x)
+            second(x - GHOST)
+
+    send_edge(1, 0, first_ref)
     take_ghosts(0, 1, u_ref)
     pl.loop(depth - 2 * GHOST, depth, step=XSTEP)(first_x)
-    send_edge(1, 0, first_ref)
     send_edge(1, 1, first_ref)
-    pl.loop(0, depth, step=2)(both)
+    pl.loop(depth - 3 * GHOST, depth, step=2)(second)
     take_ghosts(1, 0, first_ref)
     take_ghosts(1, 1, first_ref)
-    begin_x()
-    pl.loop(0, depth, step=XSTEP)(last_x)
+    begin_x(q_two_ref)
+    pl.loop(0, depth, step=LAST_XSTEP)(last_x)
 
 
 def body(cell_state, swap_slots, neighbours):
@@ -390,6 +397,8 @@
     tile = (8, 128)
     scratch = [
         (fields, depth) + pair,
+        (fields, depth) + pair,
+        (fields, depth + 2 * GHOST) + pair,
         (fields, depth) + pair,
         (fields, depth + 2 * GHOST) + pair,
         (fields, depth) + pair,

time: 65.9 us -> 62.8 us (0.953)
  Pallas kernels: 62.2 us -> 58.5 us
    pallas_call x1, Pallas kernels: 62.2 us -> 58.5 us  [body(): pl.pallas_call(functools.partial(step_kernel, n), out_shape=jax.ShapeDtyp...]
where the time goes in v6:
time: 62.8 us; the launch traced here: 62 us
  Pallas kernels  58.5 us (93%)
  local copies, waits for them, and re-layouts  2.85 us (5%)
  between operations  0.68 us (1%)
    pallas_call x1, Pallas kernels, body(): pl.pallas_call(functools.partial(step_kernel, n), out_shape=jax.ShapeDtyp...  58.5 us
    unnamed x3, local copies, waits for them, and re-layouts  1.59 us

profile of v6, /device:TPU:0, one launch (start us, length us, event | category | flops | bytes accessed | tf_op | source)
XLA Modules:
  0.0 62.0 jit_solution(7974543097526359132)
XLA Ops:
  0.7 0.0 copy-start
  0.7 1.6 %copy.4 = f32[40,8,8,128]{3,2,1,0:T(8,128)S(1)} copy(f32[40,8,8,128]{3,1,2,0:T(8,128)} %bitcast.8) | data formatting | bytes 2621440
  2.3 0.0 copy-done
  2.3 58.5 %shard_map.37 = f32[2,5,32,8,128]{4,3,2,1,0:T(8,128)S(1)} custom-call(s32[1]{0:T(128)S(6)} %copy.5.swap_ref, s32[2,3]{1,0:T(2,128)S(1)} %copy-done, f32[2,5,32,8,128]{4,3,2,1,0:T(8,128)S(1)} %bitcast.7), custom_call_target="tpu_custom_call" | custom-call | tf_op jit(solution)/shard_map/pallas_call | solution.py:418
  60.8 1.3 %reshape.7 = f32[2,5,32,1024]{3,2,1,0:T(8,128)} reshape(f32[2,5,32,8,128]{4,3,2,1,0:T(8,128)S(1)} %shard_map.37) | data formatting | bytes 2621440 | tf_op jit(solution)/shard_map/reshape | solution.py:429
Async XLA Ops:
  0.7 1.6 %copy-start = (s32[2,3]{1,0:T(2,128)S(1)}, s32[2,3]{1,0:T(2,128)}, u32[]{:S(2)}) copy-start(s32[2,3]{1,0:T(2,128)} %next_ref.1) | copy-start | bytes 76

commit v7 on v6

--- a/solution.py
+++ b/solution.py
@@ -71,14 +71,15 @@
     floor_p = 0.1 * jnp.minimum(p_l, p_r)
     guess = (c_r * p_l + c_l * p_r + c_l * c_r * (u_l - u_r)) * rcp(c_l + c_r)
     guess = jnp.maximum(guess, floor_p)
+    apart = u_r - u_l
+    half_l, half_r = 0.5 * c2_l, 0.5 * c2_r
     for _ in range(RIEMANN_ITERS):
         i_l = lax.rsqrt(a_l + b_l * guess)
         i_r = lax.rsqrt(a_r + b_r * guess)
-        star_l = u_l - (guess - p_l) * i_l
-        star_r = u_r + (guess - p_r) * i_r
-        y_l = i_l + i_l * (c2_l * (i_l * i_l))
-        y_r = i_r + i_r * (c2_r * (i_r * i_r))
-        guess = jnp.maximum(guess - 2.0 * (star_r - star_l) * rcp(y_l + y_r), floor_p)
+        gap = apart + (guess - p_r) * i_r + (guess - p_l) * i_l
+        y_l = i_l * (0.5 + half_l * (i_l * i_l))
+        y_r = i_r * (0.5 + half_r * (i_r * i_r))
+        guess = jnp.maximum(guess - gap * rcp(y_l + y_r), floor_p)
     w2_l = a_l + b_l * guess
     w2_r = a_r + b_r * guess
     w_l = w2_l * lax.rsqrt(w2_l)
@@ -104,26 +105,36 @@
     return [mass] + momenta + [mass * (inner + 0.5 * kinetic) + u * guess]
 
 
-def z_shift(x, n):
-    z = lax.broadcasted_iota(jnp.int32, x.shape, x.ndim - 1) % BZC
-    inside = pltpu.roll(x, (-n) % 128, x.ndim - 1)
-    around = pltpu.roll(x, ((BZC if n > 0 else -BZC) - n) % 128, x.ndim - 1)
-    keep = z < BZC - n if n > 0 else z >= -n
-    return jnp.where(keep, inside, around)
-
-
-def y_shift(x, n):
-    lane = lax.broadcasted_iota(jnp.int32, x.shape, 2)
-    row = lax.broadcasted_iota(jnp.int32, x.shape, 1)
-    turned = pltpu.roll(x, (-n * BZC) % 128, 2)
-    moved = pltpu.roll(turned, 7 if n > 0 else 1, 1)
-    other = jnp.concatenate([moved[i ^ 1][None] for i in range(x.shape[0])], axis=0)
-    carry = jnp.where(row == (7 if n > 0 else 0), other, moved)
-    keep = lane < 128 - n * BZC if n > 0 else lane >= -n * BZC
-    return jnp.where(keep, turned, carry)
-
-
-def plane_sweep(q, shift, axis):
+def z_shift(shape):
+    z = lax.broadcasted_iota(jnp.int32, shape, 2) & (BZC - 1)
+    keep = {1: z < BZC - 1, -1: z >= 1, -2: z >= 2}
+
+    def shift(x, n):
+        inside = pltpu.roll(x, (-n) % 128, 2)
+        around = pltpu.roll(x, ((BZC if n > 0 else -BZC) - n) % 128, 2)
+        return jnp.where(keep[n], inside, around)
+
+    return shift
+
+
+def y_shift(shape):
+    lane = lax.broadcasted_iota(jnp.int32, shape, 2)
+    row = lax.broadcasted_iota(jnp.int32, shape, 1)
+    keep = {1: lane < 128 - BZC, -1: lane >= BZC, -2: lane >= 2 * BZC}
+    first, last = row == 0, row == 7
+
+    def shift(x, n):
+        turned = pltpu.roll(x, (-n * BZC) % 128, 2)
+        moved = pltpu.roll(turned, 7 if n > 0 else 1, 1)
+        other = jnp.concatenate([moved[i ^ 1][None] for i in range(shape[0])], axis=0)
+        carry = jnp.where(last if n > 0 else first, other, moved)
+        return jnp.where(keep[n], turned, carry)
+
+    return shift
+
+
+def plane_sweep(q, shift_of, axis):
+    shift = shift_of(q[0].shape)
     d = [shift(x, 1) - x for x in q]
     d_low = [shift(x, -1) for x in d]
     d_high = [shift(x, 1) for x in d]

time: 62.8 us -> 62.7 us (level)
  no operation moved by 1% of the time
where the time goes in v7:
time: 62.7 us; the launch traced here: 61.9 us
  Pallas kernels  58.4 us (93%)
  local copies, waits for them, and re-layouts  2.85 us (5%)
  between operations  0.68 us (1%)
    pallas_call x1, Pallas kernels, body(): pl.pallas_call(functools.partial(step_kernel, n), out_shape=jax.ShapeDtyp...  58.4 us
    unnamed x3, local copies, waits for them, and re-layouts  1.59 us

profile of v7, /device:TPU:0, one launch (start us, length us, event | category | flops | bytes accessed | tf_op | source)
XLA Modules:
  0.0 61.9 jit_solution(13095863324831053480)
XLA Ops:
  0.7 0.0 copy-start
  0.7 1.6 %copy.4 = f32[40,8,8,128]{3,2,1,0:T(8,128)S(1)} copy(f32[40,8,8,128]{3,1,2,0:T(8,128)} %bitcast.8) | data formatting | bytes 2621440
  2.3 0.0 copy-done
  2.3 58.4 %shard_map.37 = f32[2,5,32,8,128]{4,3,2,1,0:T(8,128)S(1)} custom-call(s32[1]{0:T(128)S(6)} %copy.5.swap_ref, s32[2,3]{1,0:T(2,128)S(1)} %copy-done, f32[2,5,32,8,128]{4,3,2,1,0:T(8,128)S(1)} %bitcast.7), custom_call_target="tpu_custom_call" | custom-call | tf_op jit(solution)/shard_map/pallas_call | solution.py:429
  60.6 1.3 %reshape.7 = f32[2,5,32,1024]{3,2,1,0:T(8,128)} reshape(f32[2,5,32,8,128]{4,3,2,1,0:T(8,128)S(1)} %shard_map.37) | data formatting | bytes 2621440 | tf_op jit(solution)/shard_map/reshape | solution.py:440
Async XLA Ops:
  0.7 1.6 %copy-start = (s32[2,3]{1,0:T(2,128)S(1)}, s32[2,3]{1,0:T(2,128)}, u32[]{:S(2)}) copy-start(s32[2,3]{1,0:T(2,128)} %next_ref.1) | copy-start | bytes 76

commit v8 on v7

--- a/solution.py
+++ b/solution.py
@@ -12,7 +12,7 @@
 RIEMANN_ITERS = 3
 COURANT = 0.4
 XSTEP = 2
-IN_FLIGHT = 3
+IN_FLIGHT = 2
 LAST_XSTEP = 4
 
 

time: 62.7 us -> 62 us (0.989)
  no operation moved by 1% of the time
where the time goes in v8:
time: 62 us; the launch traced here: 61.6 us
  Pallas kernels  58.1 us (94%)
  local copies, waits for them, and re-layouts  2.85 us (5%)
  between operations  0.68 us (1%)
    pallas_call x1, Pallas kernels, body(): pl.pallas_call(functools.partial(step_kernel, n), out_shape=jax.ShapeDtyp...  58.1 us
    unnamed x3, local copies, waits for them, and re-layouts  1.59 us
    reshape x1, local copies, waits for them, and re-layouts, body(): return new.reshape(cell_state.shape)  1.25 us

profile of v8, /device:TPU:0, one launch (start us, length us, event | category | flops | bytes accessed | tf_op | source)
XLA Modules:
  0.0 61.6 jit_solution(10685953381070137590)
XLA Ops:
  0.7 0.0 copy-start
  0.7 1.6 %copy.4 = f32[40,8,8,128]{3,2,1,0:T(8,128)S(1)} copy(f32[40,8,8,128]{3,1,2,0:T(8,128)} %bitcast.8) | data formatting | bytes 2621440
  2.3 0.0 copy-done
  2.3 58.1 %shard_map.37 = f32[2,5,32,8,128]{4,3,2,1,0:T(8,128)S(1)} custom-call(s32[1]{0:T(128)S(6)} %copy.5.swap_ref, s32[2,3]{1,0:T(2,128)S(1)} %copy-done, f32[2,5,32,8,128]{4,3,2,1,0:T(8,128)S(1)} %bitcast.7), custom_call_target="tpu_custom_call" | custom-call | tf_op jit(solution)/shard_map/pallas_call | solution.py:429
  60.4 1.3 %reshape.7 = f32[2,5,32,1024]{3,2,1,0:T(8,128)} reshape(f32[2,5,32,8,128]{4,3,2,1,0:T(8,128)S(1)} %shard_map.37) | data formatting | bytes 2621440 | tf_op jit(solution)/shard_map/reshape | solution.py:440
Async XLA Ops:
  0.7 1.6 %copy-start = (s32[2,3]{1,0:T(2,128)S(1)}, s32[2,3]{1,0:T(2,128)}, u32[]{:S(2)}) copy-start(s32[2,3]{1,0:T(2,128)} %next_ref.1) | copy-start | bytes 76
